TPU v7x, 256 devices: a whole 4x4x8 slice. The times are simulated.
256 devices in a mesh: dp: 64 (over y, z, x_hi), mp: 4 (over x_lo, core).
Axes of the slice: x: 4 (x_hi: 2, x_lo: 2; x = x_hi * 2 + x_lo), y: 4, z: 8, core: 2. Of those that a mesh axis runs over, the one named last changes fastest.
Arguments:
- queries: bfloat16 [8192, 8192], P('dp', 'mp'), may hold values from -8 to 8
- response_keys: bfloat16 [8192, 1024], P('dp', 'mp'), may hold values from -6 to 6
- response_values: bfloat16 [8192, 1024], P('dp', 'mp'), may hold values from -6 to 6
- prompt_keys: bfloat16 [4096, 1024], P('dp', 'mp'), may hold values from -6 to 6
- prompt_value_rows: bfloat16 [4096, 1024], P('dp', 'mp'), may hold values from -6 to 6
- readout: bfloat16 [8192, 8192], P('dp', 'mp'), may hold values from -0.1875 to 0.1875
- prox_logp: float32 [8192], P('dp'), may hold values from -1.75 to 1.75
- behave_logp: float32 [8192], P('dp'), may hold values from -1.75 to 1.75
- advantage: float32 [64], P('dp'), may hold values from -6 to 6
- lengths: int32 [64], P('dp'), may hold values from 1 to 128, 4096 in all
- loss_mask: int32 [8192], P('dp'), may hold values 0 or 1
Outputs:
- grad_queries: bfloat16 [8192, 8192], P('dp', 'mp')
- response_key_gradient: bfloat16 [8192, 1024], P('dp', 'mp')
- response_value_gradient: bfloat16 [8192, 1024], P('dp', 'mp')
- prompt_key_gradient: bfloat16 [4096, 1024], P('dp', 'mp')
- prompt_value_gradient: bfloat16 [4096, 1024], P('dp', 'mp')
- response_loss_terms: float32 [64], P('dp')
Inputs may be any that keep to these rules, and one draw needn't show every extreme that they name: Response j holds real tokens in slots t < lengths[j]; some response has all 128.
All inputs are finite; a program needn't handle non-finite values. No bound on the sum of `lengths` or of `loss_mask` on one device may be relied on, other than what follows from the above.
Results may differ from a plain program's by a relative error of at most 0.012.
The roundings to bfloat16 on the way count: a program that leaves them out, or rounds other values in their place, can miss the bound.
Values may be sent and summed in bfloat16 or wider, within the bound.
A program may use at most 64 MiB of HBM per device.

v0:
```python
import math

import jax
import jax.numpy as jnp
from jax import lax
from jax.sharding import PartitionSpec as P

HEAD_SIZE = 128


clip_width = 0.2


def shifted(block, axis, distance):
    devices = range(lax.axis_size(axis))
    route = [((i - distance) % len(devices), i) for i in devices]
    return lax.ppermute(block, axis, route)


def allowed_mask(query_rows, prompt_len):
    key_ids = lax.broadcasted_iota(jnp.int32, (query_rows, prompt_len + query_rows), 1)
    query_ids = lax.broadcasted_iota(jnp.int32, (query_rows, prompt_len + query_rows), 0)
    return (key_ids < prompt_len) | (key_ids - prompt_len <= query_ids)


def policy_terms(log_prob, prox_part, behave_part, adv_value, valid, length_value, row_count):
    prob_ratio = jnp.exp(log_prob - prox_part)
    importance = jnp.exp(prox_part - behave_part)
    squashed = jnp.tanh((prob_ratio - 1.0) / clip_width)
    clipped = 1.0 + clip_width * squashed
    token_scale = jnp.where(valid, row_count / length_value, 0.0)
    objective = jnp.minimum(prob_ratio * adv_value, clipped * adv_value)
    response_loss_terms = -jnp.sum(token_scale * importance * objective)
    clip_slope = jnp.where(adv_value * (prob_ratio - 1.0) > 0, 1.0 - squashed * squashed, 1.0)
    grad_logprob = -token_scale * importance * adv_value * prob_ratio * clip_slope
    return (response_loss_terms, grad_logprob)


def per_device(
    queries,
    response_keys,
    response_values,
    prompt_keys,
    prompt_value_rows,
    readout,
    prox_logp,
    behave_logp,
    advantage,
    lengths,
    loss_mask,
):
    row_count = queries.shape[0]
    kv_width = response_keys.shape[1]
    kv_heads = kv_width // HEAD_SIZE
    head_groups = queries.shape[1] // kv_width
    half_groups = head_groups // 2
    item_count = kv_heads * 2
    score_scale = 1.0 / math.sqrt(HEAD_SIZE)
    dp_count = lax.axis_size("dp")
    stretch_len = min(16, dp_count)
    prompt_count = dp_count // stretch_len
    dp_index = lax.axis_index("dp")
    group_pos = dp_index // prompt_count
    block_rows = prompt_keys.shape[0]
    prompt_len = block_rows * stretch_len
    piled_rows = jnp.stack([prompt_keys, prompt_value_rows])
    holder = jnp.zeros((2, stretch_len, block_rows, kv_width), jnp.bfloat16)
    holder = lax.dynamic_update_index_in_dim(holder, piled_rows, group_pos, 1)

    def pass_block(step, carry):
        moving, collected = carry
        moving = shifted(moving, "dp", prompt_count)
        source = (group_pos - 1 - step) % stretch_len
        collected = lax.dynamic_update_index_in_dim(collected, moving, source, 1)
        return (moving, collected)

    _, holder = lax.fori_loop(0, stretch_len - 1, pass_block, (piled_rows, holder))
    prompt_pair = holder.reshape(2, prompt_len, kv_width)
    key_count = prompt_len + row_count
    every_key = jnp.concatenate([prompt_pair[0], response_keys], 0).reshape(
        key_count, kv_heads, HEAD_SIZE
    )
    every_value = jnp.concatenate([prompt_pair[1], response_values], 0).reshape(
        key_count, kv_heads, HEAD_SIZE
    )
    query_items = queries.reshape(row_count, item_count, half_groups, HEAD_SIZE)
    read_items = readout.reshape(row_count, item_count, half_groups, HEAD_SIZE)
    allowed = allowed_mask(row_count, prompt_len)

    def item_slices(item):
        query_item = lax.dynamic_index_in_dim(query_items, item, 1, keepdims=False)
        read_item = lax.dynamic_index_in_dim(read_items, item, 1, keepdims=False)
        key_item = lax.dynamic_index_in_dim(every_key, item // 2, 1, keepdims=False)
        value_item = lax.dynamic_index_in_dim(every_value, item // 2, 1, keepdims=False)
        return (query_item, read_item, key_item, value_item)

    def item_scores(query_item, key_item):
        scores = (
            jnp.einsum("rgd,nd->grn", query_item, key_item, preferred_element_type=jnp.float32)
            * score_scale
        )
        return jnp.where(allowed[None], scores, -jnp.inf)

    def forward_item(item):
        query_item, read_item, key_item, value_item = item_slices(item)
        scores = item_scores(query_item, key_item)
        maxima = jnp.max(scores, axis=-1, keepdims=True)
        log_total = maxima + jnp.log(jnp.sum(jnp.exp(scores - maxima), axis=-1, keepdims=True))
        probs_half = jnp.exp(scores - log_total).astype(jnp.bfloat16)
        attended = jnp.einsum(
            "grn,nd->rgd", probs_half, value_item, preferred_element_type=jnp.float32
        )
        head_dot = jnp.sum(read_item.astype(jnp.float32) * attended, axis=-1)
        return (head_dot, log_total)

    item_ids = jnp.arange(item_count, dtype=jnp.int32)
    head_dots, log_totals = lax.map(forward_item, item_ids)
    log_prob = lax.psum(jnp.sum(head_dots, axis=(0, 2)), "mp")
    valid = (jnp.arange(row_count, dtype=jnp.int32) < lengths[0]) & (loss_mask == 1)
    response_loss_terms, grad_logprob = policy_terms(
        log_prob,
        prox_logp,
        behave_logp,
        advantage[0],
        valid,
        lengths[0].astype(jnp.float32),
        row_count,
    )

    def backward_item(item):
        query_item, read_item, key_item, value_item = item_slices(item)
        head_dot = lax.dynamic_index_in_dim(head_dots, item, 0, keepdims=False)
        log_total = lax.dynamic_index_in_dim(log_totals, item, 0, keepdims=False)
        scores = item_scores(query_item, key_item)
        soft_probs = jnp.exp(scores - log_total)
        probs_half = soft_probs.astype(jnp.bfloat16)
        grad_out = (grad_logprob[:, None, None] * read_item.astype(jnp.float32)).astype(
            jnp.bfloat16
        )
        row_delta = jnp.transpose(grad_logprob[:, None] * head_dot, (1, 0))
        grad_probs = jnp.einsum(
            "rgd,nd->grn", grad_out, value_item, preferred_element_type=jnp.float32
        )
        grad_scores = (soft_probs * (grad_probs - row_delta[:, :, None])).astype(jnp.bfloat16)
        query_gradient = (
            jnp.einsum("grn,nd->rgd", grad_scores, key_item, preferred_element_type=jnp.float32)
            * score_scale
        ).astype(jnp.bfloat16)
        key_gradient = (
            jnp.einsum("grn,rgd->nd", grad_scores, query_item, preferred_element_type=jnp.float32)
            * score_scale
        )
        value_gradient = jnp.einsum(
            "grn,rgd->nd", probs_half, grad_out, preferred_element_type=jnp.float32
        )
        return (query_gradient, key_gradient, value_gradient)

    grad_query_items, grad_key_items, grad_value_items = lax.map(backward_item, item_ids)
    grad_queries = jnp.transpose(grad_query_items, (1, 0, 2, 3)).reshape(
        row_count, queries.shape[1]
    )
    key_grads = jnp.transpose(
        grad_key_items.reshape(kv_heads, 2, key_count, HEAD_SIZE).sum(axis=1), (1, 0, 2)
    ).reshape(key_count, kv_width)
    value_grads = jnp.transpose(
        grad_value_items.reshape(kv_heads, 2, key_count, HEAD_SIZE).sum(axis=1), (1, 0, 2)
    ).reshape(key_count, kv_width)
    prompt_grad = jnp.stack([key_grads[:prompt_len], value_grads[:prompt_len]])
    term_blocks = prompt_grad.reshape(2, stretch_len, block_rows, kv_width)

    def add_block(step, running):
        incoming = shifted(running, "dp", prompt_count)
        target = (group_pos - 2 - step) % stretch_len
        return incoming + lax.dynamic_index_in_dim(term_blocks, target, 1, keepdims=False)

    first_block = lax.dynamic_index_in_dim(
        term_blocks, (group_pos - 1) % stretch_len, 1, keepdims=False
    )
    own_rows = lax.fori_loop(0, stretch_len - 1, add_block, first_block)
    return (
        grad_queries,
        key_grads[prompt_len:].astype(jnp.bfloat16),
        value_grads[prompt_len:].astype(jnp.bfloat16),
        own_rows[0].astype(jnp.bfloat16),
        own_rows[1].astype(jnp.bfloat16),
        response_loss_terms.reshape(1),
    )


def solution(mesh):
    placed = (
        P("dp", "mp"),
        P("dp", "mp"),
        P("dp", "mp"),
        P("dp", "mp"),
        P("dp", "mp"),
        P("dp", "mp"),
        P("dp"),
        P("dp"),
        P("dp"),
        P("dp"),
        P("dp"),
    )
    return jax.shard_map(
        per_device,
        mesh=mesh,
        in_specs=placed,
        out_specs=(
            P("dp", "mp"),
            P("dp", "mp"),
            P("dp", "mp"),
            P("dp", "mp"),
            P("dp", "mp"),
            P("dp"),
        ),
        check_vma=False,
    )
```

profile of v0, /device:TPU:4, one launch (start us, length us, event | category | flops | bytes accessed | tf_op | source)
XLA Modules:
  0.0 463.8 jit_solution(12488414801425036122)
XLA Ops:
  2.3 133.4 %while.64 = (s32[]{:T(128)}, bf16[2,64,256]{2,1,0:T(8,128)(2,1)S(1)}, bf16[2,16,64,256]{3,2,0,1:T(8,128)(2,1)S(1)}, s32[]{:T(128)}, s32[]{:T(128)}, /*index=5*/s32[]{:T(128)}, s32[]{:T(128)}, s32[]{:T(128)}) while((s32[]{:T(128)}, bf16[2,64,256]{2,1,0:T(8,128)(2,1)S(1)}, bf16[2,16,64,256]{3,2,0,1:T(8,128)(2,1)S(1)}, s32[]{:T(128)}, s32[]{:T(128)}, ...), condition=%wide.region_1.2_spmd, body=%wide.region_0.1_spmd.sunk | while | flops 17 | bytes 524572 | solution.py:77
  13.6 8.9 %collective-permute-done = bf16[2,64,256]{2,1,0:T(8,128)(2,1)S(1)} collective-permute-done((bf16[2,64,256]{2,1,0:T(8,128)(2,1)S(1)}, bf16[2,64,256]{2,1,0:T(8,128)(2,1)S(1)}, u32[]{:S(2)}, u32[]{:S(2)}) %collective-permute-start) | collective-permute-done | bytes 65568 | tf_op jit(solution)/shard_map/while/body/eval_jaxpr/ppermute | solution.py:17
  22.6 8.4 %collective-permute-done = bf16[2,64,256]{2,1,0:T(8,128)(2,1)S(1)} collective-permute-done((bf16[2,64,256]{2,1,0:T(8,128)(2,1)S(1)}, bf16[2,64,256]{2,1,0:T(8,128)(2,1)S(1)}, u32[]{:S(2)}, u32[]{:S(2)}) %collective-permute-start) | collective-permute-done | bytes 65568 | tf_op jit(solution)/shard_map/while/body/eval_jaxpr/ppermute | solution.py:17
  31.2 8.5 %collective-permute-done = bf16[2,64,256]{2,1,0:T(8,128)(2,1)S(1)} collective-permute-done((bf16[2,64,256]{2,1,0:T(8,128)(2,1)S(1)}, bf16[2,64,256]{2,1,0:T(8,128)(2,1)S(1)}, u32[]{:S(2)}, u32[]{:S(2)}) %collective-permute-start) | collective-permute-done | bytes 65568 | tf_op jit(solution)/shard_map/while/body/eval_jaxpr/ppermute | solution.py:17
  39.8 8.4 %collective-permute-done = bf16[2,64,256]{2,1,0:T(8,128)(2,1)S(1)} collective-permute-done((bf16[2,64,256]{2,1,0:T(8,128)(2,1)S(1)}, bf16[2,64,256]{2,1,0:T(8,128)(2,1)S(1)}, u32[]{:S(2)}, u32[]{:S(2)}) %collective-permute-start) | collective-permute-done | bytes 65568 | tf_op jit(solution)/shard_map/while/body/eval_jaxpr/ppermute | solution.py:17
  48.4 8.8 %collective-permute-done = bf16[2,64,256]{2,1,0:T(8,128)(2,1)S(1)} collective-permute-done((bf16[2,64,256]{2,1,0:T(8,128)(2,1)S(1)}, bf16[2,64,256]{2,1,0:T(8,128)(2,1)S(1)}, u32[]{:S(2)}, u32[]{:S(2)}) %collective-permute-start) | collective-permute-done | bytes 65568 | tf_op jit(solution)/shard_map/while/body/eval_jaxpr/ppermute | solution.py:17
  57.3 8.5 %collective-permute-done = bf16[2,64,256]{2,1,0:T(8,128)(2,1)S(1)} collective-permute-done((bf16[2,64,256]{2,1,0:T(8,128)(2,1)S(1)}, bf16[2,64,256]{2,1,0:T(8,128)(2,1)S(1)}, u32[]{:S(2)}, u32[]{:S(2)}) %collective-permute-start) | collective-permute-done | bytes 65568 | tf_op jit(solution)/shard_map/while/body/eval_jaxpr/ppermute | solution.py:17
  66.0 8.5 %collective-permute-done = bf16[2,64,256]{2,1,0:T(8,128)(2,1)S(1)} collective-permute-done((bf16[2,64,256]{2,1,0:T(8,128)(2,1)S(1)}, bf16[2,64,256]{2,1,0:T(8,128)(2,1)S(1)}, u32[]{:S(2)}, u32[]{:S(2)}) %collective-permute-start) | collective-permute-done | bytes 65568 | tf_op jit(solution)/shard_map/while/body/eval_jaxpr/ppermute | solution.py:17
  74.6 8.5 %collective-permute-done = bf16[2,64,256]{2,1,0:T(8,128)(2,1)S(1)} collective-permute-done((bf16[2,64,256]{2,1,0:T(8,128)(2,1)S(1)}, bf16[2,64,256]{2,1,0:T(8,128)(2,1)S(1)}, u32[]{:S(2)}, u32[]{:S(2)}) %collective-permute-start) | collective-permute-done | bytes 65568 | tf_op jit(solution)/shard_map/while/body/eval_jaxpr/ppermute | solution.py:17
  83.3 8.4 %collective-permute-done = bf16[2,64,256]{2,1,0:T(8,128)(2,1)S(1)} collective-permute-done((bf16[2,64,256]{2,1,0:T(8,128)(2,1)S(1)}, bf16[2,64,256]{2,1,0:T(8,128)(2,1)S(1)}, u32[]{:S(2)}, u32[]{:S(2)}) %collective-permute-start) | collective-permute-done | bytes 65568 | tf_op jit(solution)/shard_map/while/body/eval_jaxpr/ppermute | solution.py:17
  91.9 8.4 %collective-permute-done = bf16[2,64,256]{2,1,0:T(8,128)(2,1)S(1)} collective-permute-done((bf16[2,64,256]{2,1,0:T(8,128)(2,1)S(1)}, bf16[2,64,256]{2,1,0:T(8,128)(2,1)S(1)}, u32[]{:S(2)}, u32[]{:S(2)}) %collective-permute-start) | collective-permute-done | bytes 65568 | tf_op jit(solution)/shard_map/while/body/eval_jaxpr/ppermute | solution.py:17
  100.5 9.2 %collective-permute-done = bf16[2,64,256]{2,1,0:T(8,128)(2,1)S(1)} collective-permute-done((bf16[2,64,256]{2,1,0:T(8,128)(2,1)S(1)}, bf16[2,64,256]{2,1,0:T(8,128)(2,1)S(1)}, u32[]{:S(2)}, u32[]{:S(2)}) %collective-permute-start) | collective-permute-done | bytes 65568 | tf_op jit(solution)/shard_map/while/body/eval_jaxpr/ppermute | solution.py:17
  109.8 8.7 %collective-permute-done = bf16[2,64,256]{2,1,0:T(8,128)(2,1)S(1)} collective-permute-done((bf16[2,64,256]{2,1,0:T(8,128)(2,1)S(1)}, bf16[2,64,256]{2,1,0:T(8,128)(2,1)S(1)}, u32[]{:S(2)}, u32[]{:S(2)}) %collective-permute-start) | collective-permute-done | bytes 65568 | tf_op jit(solution)/shard_map/while/body/eval_jaxpr/ppermute | solution.py:17
  118.7 8.4 %collective-permute-done = bf16[2,64,256]{2,1,0:T(8,128)(2,1)S(1)} collective-permute-done((bf16[2,64,256]{2,1,0:T(8,128)(2,1)S(1)}, bf16[2,64,256]{2,1,0:T(8,128)(2,1)S(1)}, u32[]{:S(2)}, u32[]{:S(2)}) %collective-permute-start) | collective-permute-done | bytes 65568 | tf_op jit(solution)/shard_map/while/body/eval_jaxpr/ppermute | solution.py:17
  146.6 39.0 %while.66 = (s32[]{:T(128)}, f32[4,128,4]{1,2,0:T(4,128)}, f32[4,4,128,1]{2,1,3,0:T(4,128)}, s32[4]{0:T(128)S(1)}, bf16[128,4,4,128]{0,3,2,1:T(8,128)(2,1)}, /*i...) while((s32[]{:T(128)}, f32[4,128,4]{1,2,0:T(4,128)}, ...), condition=%wide.region_6.7_spmd.clone, body=%wide.region_2.6_spmd.clone.sunk | while | flops 306609152 | bytes 8254458 | solution.py:117
  195.1 61.6 %while.67 = (s32[]{:T(128)}, bf16[4,128,4,128]{1,3,2,0:T(8,128)(2,1)}, f32[4,1152,128]{2,1,0:T(8,128)}, f32[4,1152,128]{2,1,0:T(8,128)}, s32[4]{0:T(128)S(1)}, /...) while((s32[]{:T(128)}, ...), condition=%wide.region_10.11_spmd.clone, body=%wide.region_9.10_spmd.clone.sunk | while | flops 760070656 | bytes 14177322 | solution.py:158
  270.7 186.9 %while.65 = (s32[]{:T(128)}, f32[2,64,256]{2,1,0:T(8,128)S(1)}, s32[]{:T(128)}, f32[2,16,64,256]{3,2,1,0:T(8,128)}, s32[]{:T(128)}, /*index=5*/s32[]{:T(128)}, s32[]{:T(128)}, s32[]{:T(128)}) while((s32[]{:T(128)}, f32[2,64,256]{2,1,0:T(8,128)S(1)}, s32[]{:T(128)}, f32[2,16,64,256]{3,2,1,0:T(8,128)}, s32[]{:T(128)}, /*index=5*/s32[]{:T(128)}, ...), condition=%wide.region_14.15_spmd, body=%wide.region_13.14_spmd.sunk | while | flops 32785 | bytes 917788 | solution.py:179
  270.8 9.6 %collective-permute-done.1 = f32[2,64,256]{2,1,0:T(8,128)S(1)} collective-permute-done((f32[2,64,256]{2,1,0:T(8,128)S(1)}, f32[2,64,256]{2,1,0:T(8,128)S(1)}, u32[]{:S(2)}, u32[]{:S(2)}) %collective-permute-start.1) | collective-permute-done | bytes 131104 | tf_op jit(solution)/shard_map/while/body/eval_jaxpr/ppermute | solution.py:17
  281.5 10.7 %collective-permute-done.1 = f32[2,64,256]{2,1,0:T(8,128)S(1)} collective-permute-done((f32[2,64,256]{2,1,0:T(8,128)S(1)}, f32[2,64,256]{2,1,0:T(8,128)S(1)}, u32[]{:S(2)}, u32[]{:S(2)}) %collective-permute-start.1) | collective-permute-done | bytes 131104 | tf_op jit(solution)/shard_map/while/body/eval_jaxpr/ppermute | solution.py:17
  293.3 12.2 %collective-permute-done.1 = f32[2,64,256]{2,1,0:T(8,128)S(1)} collective-permute-done((f32[2,64,256]{2,1,0:T(8,128)S(1)}, f32[2,64,256]{2,1,0:T(8,128)S(1)}, u32[]{:S(2)}, u32[]{:S(2)}) %collective-permute-start.1) | collective-permute-done | bytes 131104 | tf_op jit(solution)/shard_map/while/body/eval_jaxpr/ppermute | solution.py:17
  306.6 12.1 %collective-permute-done.1 = f32[2,64,256]{2,1,0:T(8,128)S(1)} collective-permute-done((f32[2,64,256]{2,1,0:T(8,128)S(1)}, f32[2,64,256]{2,1,0:T(8,128)S(1)}, u32[]{:S(2)}, u32[]{:S(2)}) %collective-permute-start.1) | collective-permute-done | bytes 131104 | tf_op jit(solution)/shard_map/while/body/eval_jaxpr/ppermute | solution.py:17
  319.7 12.1 %collective-permute-done.1 = f32[2,64,256]{2,1,0:T(8,128)S(1)} collective-permute-done((f32[2,64,256]{2,1,0:T(8,128)S(1)}, f32[2,64,256]{2,1,0:T(8,128)S(1)}, u32[]{:S(2)}, u32[]{:S(2)}) %collective-permute-start.1) | collective-permute-done | bytes 131104 | tf_op jit(solution)/shard_map/while/body/eval_jaxpr/ppermute | solution.py:17
  332.9 12.4 %collective-permute-done.1 = f32[2,64,256]{2,1,0:T(8,128)S(1)} collective-permute-done((f32[2,64,256]{2,1,0:T(8,128)S(1)}, f32[2,64,256]{2,1,0:T(8,128)S(1)}, u32[]{:S(2)}, u32[]{:S(2)}) %collective-permute-start.1) | collective-permute-done | bytes 131104 | tf_op jit(solution)/shard_map/while/body/eval_jaxpr/ppermute | solution.py:17
  346.3 12.3 %collective-permute-done.1 = f32[2,64,256]{2,1,0:T(8,128)S(1)} collective-permute-done((f32[2,64,256]{2,1,0:T(8,128)S(1)}, f32[2,64,256]{2,1,0:T(8,128)S(1)}, u32[]{:S(2)}, u32[]{:S(2)}) %collective-permute-start.1) | collective-permute-done | bytes 131104 | tf_op jit(solution)/shard_map/while/body/eval_jaxpr/ppermute | solution.py:17
  359.7 11.0 %collective-permute-done.1 = f32[2,64,256]{2,1,0:T(8,128)S(1)} collective-permute-done((f32[2,64,256]{2,1,0:T(8,128)S(1)}, f32[2,64,256]{2,1,0:T(8,128)S(1)}, u32[]{:S(2)}, u32[]{:S(2)}) %collective-permute-start.1) | collective-permute-done | bytes 131104 | tf_op jit(solution)/shard_map/while/body/eval_jaxpr/ppermute | solution.py:17
  371.7 9.3 %collective-permute-done.1 = f32[2,64,256]{2,1,0:T(8,128)S(1)} collective-permute-done((f32[2,64,256]{2,1,0:T(8,128)S(1)}, f32[2,64,256]{2,1,0:T(8,128)S(1)}, u32[]{:S(2)}, u32[]{:S(2)}) %collective-permute-start.1) | collective-permute-done | bytes 131104 | tf_op jit(solution)/shard_map/while/body/eval_jaxpr/ppermute | solution.py:17
  382.1 9.5 %collective-permute-done.1 = f32[2,64,256]{2,1,0:T(8,128)S(1)} collective-permute-done((f32[2,64,256]{2,1,0:T(8,128)S(1)}, f32[2,64,256]{2,1,0:T(8,128)S(1)}, u32[]{:S(2)}, u32[]{:S(2)}) %collective-permute-start.1) | collective-permute-done | bytes 131104 | tf_op jit(solution)/shard_map/while/body/eval_jaxpr/ppermute | solution.py:17
  392.6 11.2 %collective-permute-done.1 = f32[2,64,256]{2,1,0:T(8,128)S(1)} collective-permute-done((f32[2,64,256]{2,1,0:T(8,128)S(1)}, f32[2,64,256]{2,1,0:T(8,128)S(1)}, u32[]{:S(2)}, u32[]{:S(2)}) %collective-permute-start.1) | collective-permute-done | bytes 131104 | tf_op jit(solution)/shard_map/while/body/eval_jaxpr/ppermute | solution.py:17
  404.9 11.8 %collective-permute-done.1 = f32[2,64,256]{2,1,0:T(8,128)S(1)} collective-permute-done((f32[2,64,256]{2,1,0:T(8,128)S(1)}, f32[2,64,256]{2,1,0:T(8,128)S(1)}, u32[]{:S(2)}, u32[]{:S(2)}) %collective-permute-start.1) | collective-permute-done | bytes 131104 | tf_op jit(solution)/shard_map/while/body/eval_jaxpr/ppermute | solution.py:17
  417.7 12.1 %collective-permute-done.1 = f32[2,64,256]{2,1,0:T(8,128)S(1)} collective-permute-done((f32[2,64,256]{2,1,0:T(8,128)S(1)}, f32[2,64,256]{2,1,0:T(8,128)S(1)}, u32[]{:S(2)}, u32[]{:S(2)}) %collective-permute-start.1) | collective-permute-done | bytes 131104 | tf_op jit(solution)/shard_map/while/body/eval_jaxpr/ppermute | solution.py:17
  430.9 12.4 %collective-permute-done.1 = f32[2,64,256]{2,1,0:T(8,128)S(1)} collective-permute-done((f32[2,64,256]{2,1,0:T(8,128)S(1)}, f32[2,64,256]{2,1,0:T(8,128)S(1)}, u32[]{:S(2)}, u32[]{:S(2)}) %collective-permute-start.1) | collective-permute-done | bytes 131104 | tf_op jit(solution)/shard_map/while/body/eval_jaxpr/ppermute | solution.py:17
  444.3 12.3 %collective-permute-done.1 = f32[2,64,256]{2,1,0:T(8,128)S(1)} collective-permute-done((f32[2,64,256]{2,1,0:T(8,128)S(1)}, f32[2,64,256]{2,1,0:T(8,128)S(1)}, u32[]{:S(2)}, u32[]{:S(2)}) %collective-permute-start.1) | collective-permute-done | bytes 131104 | tf_op jit(solution)/shard_map/while/body/eval_jaxpr/ppermute | solution.py:17
  (212 shorter events, 144.0 us)
Async XLA Ops:
  2.3 133.6 %copy-start.2 = (bf16[128,256]{1,0:T(8,128)(2,1)S(1)}, bf16[128,256]{1,0:T(8,128)(2,1)}, u32[]{:S(2)}) copy-start(bf16[128,256]{1,0:T(8,128)(2,1)} %param.21) | copy-start | bytes 196612
  2.4 11.1 %collective-permute-start = (bf16[2,64,256]{2,1,0:T(8,128)(2,1)S(1)}, bf16[2,64,256]{2,1,0:T(8,128)(2,1)S(1)}, u32[]{:S(2)}, u32[]{:S(2)}) collective-permute-start(bf16[2,64,256]{2,1,0:T(8,128)(2,1)S(1)} %get-tuple-element.957), channel_id=1, source_target_pairs={{240,0},{244,4},{248,8},{252,12},{0,16},{4,20},{8,24},{12,28},{16,... | collective-permute-start | bytes 196616 | tf_op jit(solution)/shard_map/while/body/eval_jaxpr/ppermute | solution.py:17
  13.5 9.0 %collective-permute-start = (bf16[2,64,256]{2,1,0:T(8,128)(2,1)S(1)}, bf16[2,64,256]{2,1,0:T(8,128)(2,1)S(1)}, u32[]{:S(2)}, u32[]{:S(2)}) collective-permute-start(bf16[2,64,256]{2,1,0:T(8,128)(2,1)S(1)} %get-tuple-element.957), channel_id=1, source_target_pairs={{240,0},{244,4},{248,8},{252,12},{0,16},{4,20},{8,24},{12,28},{16,... | collective-permute-start | bytes 196616 | tf_op jit(solution)/shard_map/while/body/eval_jaxpr/ppermute | solution.py:17
  22.5 8.6 %collective-permute-start = (bf16[2,64,256]{2,1,0:T(8,128)(2,1)S(1)}, bf16[2,64,256]{2,1,0:T(8,128)(2,1)S(1)}, u32[]{:S(2)}, u32[]{:S(2)}) collective-permute-start(bf16[2,64,256]{2,1,0:T(8,128)(2,1)S(1)} %get-tuple-element.957), channel_id=1, source_target_pairs={{240,0},{244,4},{248,8},{252,12},{0,16},{4,20},{8,24},{12,28},{16,... | collective-permute-start | bytes 196616 | tf_op jit(solution)/shard_map/while/body/eval_jaxpr/ppermute | solution.py:17
  31.1 8.6 %collective-permute-start = (bf16[2,64,256]{2,1,0:T(8,128)(2,1)S(1)}, bf16[2,64,256]{2,1,0:T(8,128)(2,1)S(1)}, u32[]{:S(2)}, u32[]{:S(2)}) collective-permute-start(bf16[2,64,256]{2,1,0:T(8,128)(2,1)S(1)} %get-tuple-element.957), channel_id=1, source_target_pairs={{240,0},{244,4},{248,8},{252,12},{0,16},{4,20},{8,24},{12,28},{16,... | collective-permute-start | bytes 196616 | tf_op jit(solution)/shard_map/while/body/eval_jaxpr/ppermute | solution.py:17
  39.7 8.6 %collective-permute-start = (bf16[2,64,256]{2,1,0:T(8,128)(2,1)S(1)}, bf16[2,64,256]{2,1,0:T(8,128)(2,1)S(1)}, u32[]{:S(2)}, u32[]{:S(2)}) collective-permute-start(bf16[2,64,256]{2,1,0:T(8,128)(2,1)S(1)} %get-tuple-element.957), channel_id=1, source_target_pairs={{240,0},{244,4},{248,8},{252,12},{0,16},{4,20},{8,24},{12,28},{16,... | collective-permute-start | bytes 196616 | tf_op jit(solution)/shard_map/while/body/eval_jaxpr/ppermute | solution.py:17
  48.3 8.9 %collective-permute-start = (bf16[2,64,256]{2,1,0:T(8,128)(2,1)S(1)}, bf16[2,64,256]{2,1,0:T(8,128)(2,1)S(1)}, u32[]{:S(2)}, u32[]{:S(2)}) collective-permute-start(bf16[2,64,256]{2,1,0:T(8,128)(2,1)S(1)} %get-tuple-element.957), channel_id=1, source_target_pairs={{240,0},{244,4},{248,8},{252,12},{0,16},{4,20},{8,24},{12,28},{16,... | collective-permute-start | bytes 196616 | tf_op jit(solution)/shard_map/while/body/eval_jaxpr/ppermute | solution.py:17
  57.2 8.6 %collective-permute-start = (bf16[2,64,256]{2,1,0:T(8,128)(2,1)S(1)}, bf16[2,64,256]{2,1,0:T(8,128)(2,1)S(1)}, u32[]{:S(2)}, u32[]{:S(2)}) collective-permute-start(bf16[2,64,256]{2,1,0:T(8,128)(2,1)S(1)} %get-tuple-element.957), channel_id=1, source_target_pairs={{240,0},{244,4},{248,8},{252,12},{0,16},{4,20},{8,24},{12,28},{16,... | collective-permute-start | bytes 196616 | tf_op jit(solution)/shard_map/while/body/eval_jaxpr/ppermute | solution.py:17
  65.8 8.7 %collective-permute-start = (bf16[2,64,256]{2,1,0:T(8,128)(2,1)S(1)}, bf16[2,64,256]{2,1,0:T(8,128)(2,1)S(1)}, u32[]{:S(2)}, u32[]{:S(2)}) collective-permute-start(bf16[2,64,256]{2,1,0:T(8,128)(2,1)S(1)} %get-tuple-element.957), channel_id=1, source_target_pairs={{240,0},{244,4},{248,8},{252,12},{0,16},{4,20},{8,24},{12,28},{16,... | collective-permute-start | bytes 196616 | tf_op jit(solution)/shard_map/while/body/eval_jaxpr/ppermute | solution.py:17
  74.5 8.7 %collective-permute-start = (bf16[2,64,256]{2,1,0:T(8,128)(2,1)S(1)}, bf16[2,64,256]{2,1,0:T(8,128)(2,1)S(1)}, u32[]{:S(2)}, u32[]{:S(2)}) collective-permute-start(bf16[2,64,256]{2,1,0:T(8,128)(2,1)S(1)} %get-tuple-element.957), channel_id=1, source_target_pairs={{240,0},{244,4},{248,8},{252,12},{0,16},{4,20},{8,24},{12,28},{16,... | collective-permute-start | bytes 196616 | tf_op jit(solution)/shard_map/while/body/eval_jaxpr/ppermute | solution.py:17
  83.2 8.6 %collective-permute-start = (bf16[2,64,256]{2,1,0:T(8,128)(2,1)S(1)}, bf16[2,64,256]{2,1,0:T(8,128)(2,1)S(1)}, u32[]{:S(2)}, u32[]{:S(2)}) collective-permute-start(bf16[2,64,256]{2,1,0:T(8,128)(2,1)S(1)} %get-tuple-element.957), channel_id=1, source_target_pairs={{240,0},{244,4},{248,8},{252,12},{0,16},{4,20},{8,24},{12,28},{16,... | collective-permute-start | bytes 196616 | tf_op jit(solution)/shard_map/while/body/eval_jaxpr/ppermute | solution.py:17
  91.8 8.6 %collective-permute-start = (bf16[2,64,256]{2,1,0:T(8,128)(2,1)S(1)}, bf16[2,64,256]{2,1,0:T(8,128)(2,1)S(1)}, u32[]{:S(2)}, u32[]{:S(2)}) collective-permute-start(bf16[2,64,256]{2,1,0:T(8,128)(2,1)S(1)} %get-tuple-element.957), channel_id=1, source_target_pairs={{240,0},{244,4},{248,8},{252,12},{0,16},{4,20},{8,24},{12,28},{16,... | collective-permute-start | bytes 196616 | tf_op jit(solution)/shard_map/while/body/eval_jaxpr/ppermute | solution.py:17
  100.4 9.3 %collective-permute-start = (bf16[2,64,256]{2,1,0:T(8,128)(2,1)S(1)}, bf16[2,64,256]{2,1,0:T(8,128)(2,1)S(1)}, u32[]{:S(2)}, u32[]{:S(2)}) collective-permute-start(bf16[2,64,256]{2,1,0:T(8,128)(2,1)S(1)} %get-tuple-element.957), channel_id=1, source_target_pairs={{240,0},{244,4},{248,8},{252,12},{0,16},{4,20},{8,24},{12,28},{16,... | collective-permute-start | bytes 196616 | tf_op jit(solution)/shard_map/while/body/eval_jaxpr/ppermute | solution.py:17
  109.7 8.8 %collective-permute-start = (bf16[2,64,256]{2,1,0:T(8,128)(2,1)S(1)}, bf16[2,64,256]{2,1,0:T(8,128)(2,1)S(1)}, u32[]{:S(2)}, u32[]{:S(2)}) collective-permute-start(bf16[2,64,256]{2,1,0:T(8,128)(2,1)S(1)} %get-tuple-element.957), channel_id=1, source_target_pairs={{240,0},{244,4},{248,8},{252,12},{0,16},{4,20},{8,24},{12,28},{16,... | collective-permute-start | bytes 196616 | tf_op jit(solution)/shard_map/while/body/eval_jaxpr/ppermute | solution.py:17
  118.6 8.6 %collective-permute-start = (bf16[2,64,256]{2,1,0:T(8,128)(2,1)S(1)}, bf16[2,64,256]{2,1,0:T(8,128)(2,1)S(1)}, u32[]{:S(2)}, u32[]{:S(2)}) collective-permute-start(bf16[2,64,256]{2,1,0:T(8,128)(2,1)S(1)} %get-tuple-element.957), channel_id=1, source_target_pairs={{240,0},{244,4},{248,8},{252,12},{0,16},{4,20},{8,24},{12,28},{16,... | collective-permute-start | bytes 196616 | tf_op jit(solution)/shard_map/while/body/eval_jaxpr/ppermute | solution.py:17
  127.2 8.6 %collective-permute-start = (bf16[2,64,256]{2,1,0:T(8,128)(2,1)S(1)}, bf16[2,64,256]{2,1,0:T(8,128)(2,1)S(1)}, u32[]{:S(2)}, u32[]{:S(2)}) collective-permute-start(bf16[2,64,256]{2,1,0:T(8,128)(2,1)S(1)} %get-tuple-element.957), channel_id=1, source_target_pairs={{240,0},{244,4},{248,8},{252,12},{0,16},{4,20},{8,24},{12,28},{16,... | collective-permute-start | bytes 196616 | tf_op jit(solution)/shard_map/while/body/eval_jaxpr/ppermute | solution.py:17
  146.5 47.0 %copy-start.4 = (f32[128]{0:T(128)S(1)}, f32[128]{0:T(128)}, u32[]{:S(2)}) copy-start(f32[128]{0:T(128)} %param.25) | copy-start | bytes 1540
  270.7 9.7 %collective-permute-start.1 = (f32[2,64,256]{2,1,0:T(8,128)S(1)}, f32[2,64,256]{2,1,0:T(8,128)S(1)}, u32[]{:S(2)}, u32[]{:S(2)}) collective-permute-start(f32[2,64,256]{2,1,0:T(8,128)S(1)} %get-tuple-element.1083), channel_id=1, source_target_pairs={{240,0},{244,4},{248,8},{252,12},{0,16},{4,20},{8,24},{12,28},{16,... | collective-permute-start | bytes 393224 | tf_op jit(solution)/shard_map/while/body/eval_jaxpr/ppermute | solution.py:17
  281.4 10.9 %collective-permute-start.1 = (f32[2,64,256]{2,1,0:T(8,128)S(1)}, f32[2,64,256]{2,1,0:T(8,128)S(1)}, u32[]{:S(2)}, u32[]{:S(2)}) collective-permute-start(f32[2,64,256]{2,1,0:T(8,128)S(1)} %get-tuple-element.1083), channel_id=1, source_target_pairs={{240,0},{244,4},{248,8},{252,12},{0,16},{4,20},{8,24},{12,28},{16,... | collective-permute-start | bytes 393224 | tf_op jit(solution)/shard_map/while/body/eval_jaxpr/ppermute | solution.py:17
  293.2 12.3 %collective-permute-start.1 = (f32[2,64,256]{2,1,0:T(8,128)S(1)}, f32[2,64,256]{2,1,0:T(8,128)S(1)}, u32[]{:S(2)}, u32[]{:S(2)}) collective-permute-start(f32[2,64,256]{2,1,0:T(8,128)S(1)} %get-tuple-element.1083), channel_id=1, source_target_pairs={{240,0},{244,4},{248,8},{252,12},{0,16},{4,20},{8,24},{12,28},{16,... | collective-permute-start | bytes 393224 | tf_op jit(solution)/shard_map/while/body/eval_jaxpr/ppermute | solution.py:17
  306.4 12.3 %collective-permute-start.1 = (f32[2,64,256]{2,1,0:T(8,128)S(1)}, f32[2,64,256]{2,1,0:T(8,128)S(1)}, u32[]{:S(2)}, u32[]{:S(2)}) collective-permute-start(f32[2,64,256]{2,1,0:T(8,128)S(1)} %get-tuple-element.1083), channel_id=1, source_target_pairs={{240,0},{244,4},{248,8},{252,12},{0,16},{4,20},{8,24},{12,28},{16,... | collective-permute-start | bytes 393224 | tf_op jit(solution)/shard_map/while/body/eval_jaxpr/ppermute | solution.py:17
  319.6 12.3 %collective-permute-start.1 = (f32[2,64,256]{2,1,0:T(8,128)S(1)}, f32[2,64,256]{2,1,0:T(8,128)S(1)}, u32[]{:S(2)}, u32[]{:S(2)}) collective-permute-start(f32[2,64,256]{2,1,0:T(8,128)S(1)} %get-tuple-element.1083), channel_id=1, source_target_pairs={{240,0},{244,4},{248,8},{252,12},{0,16},{4,20},{8,24},{12,28},{16,... | collective-permute-start | bytes 393224 | tf_op jit(solution)/shard_map/while/body/eval_jaxpr/ppermute | solution.py:17
  332.8 12.5 %collective-permute-start.1 = (f32[2,64,256]{2,1,0:T(8,128)S(1)}, f32[2,64,256]{2,1,0:T(8,128)S(1)}, u32[]{:S(2)}, u32[]{:S(2)}) collective-permute-start(f32[2,64,256]{2,1,0:T(8,128)S(1)} %get-tuple-element.1083), channel_id=1, source_target_pairs={{240,0},{244,4},{248,8},{252,12},{0,16},{4,20},{8,24},{12,28},{16,... | collective-permute-start | bytes 393224 | tf_op jit(solution)/shard_map/while/body/eval_jaxpr/ppermute | solution.py:17
  346.2 12.4 %collective-permute-start.1 = (f32[2,64,256]{2,1,0:T(8,128)S(1)}, f32[2,64,256]{2,1,0:T(8,128)S(1)}, u32[]{:S(2)}, u32[]{:S(2)}) collective-permute-start(f32[2,64,256]{2,1,0:T(8,128)S(1)} %get-tuple-element.1083), channel_id=1, source_target_pairs={{240,0},{244,4},{248,8},{252,12},{0,16},{4,20},{8,24},{12,28},{16,... | collective-permute-start | bytes 393224 | tf_op jit(solution)/shard_map/while/body/eval_jaxpr/ppermute | solution.py:17
  359.6 11.1 %collective-permute-start.1 = (f32[2,64,256]{2,1,0:T(8,128)S(1)}, f32[2,64,256]{2,1,0:T(8,128)S(1)}, u32[]{:S(2)}, u32[]{:S(2)}) collective-permute-start(f32[2,64,256]{2,1,0:T(8,128)S(1)} %get-tuple-element.1083), channel_id=1, source_target_pairs={{240,0},{244,4},{248,8},{252,12},{0,16},{4,20},{8,24},{12,28},{16,... | collective-permute-start | bytes 393224 | tf_op jit(solution)/shard_map/while/body/eval_jaxpr/ppermute | solution.py:17
  371.6 9.4 %collective-permute-start.1 = (f32[2,64,256]{2,1,0:T(8,128)S(1)}, f32[2,64,256]{2,1,0:T(8,128)S(1)}, u32[]{:S(2)}, u32[]{:S(2)}) collective-permute-start(f32[2,64,256]{2,1,0:T(8,128)S(1)} %get-tuple-element.1083), channel_id=1, source_target_pairs={{240,0},{244,4},{248,8},{252,12},{0,16},{4,20},{8,24},{12,28},{16,... | collective-permute-start | bytes 393224 | tf_op jit(solution)/shard_map/while/body/eval_jaxpr/ppermute | solution.py:17
  382.0 9.6 %collective-permute-start.1 = (f32[2,64,256]{2,1,0:T(8,128)S(1)}, f32[2,64,256]{2,1,0:T(8,128)S(1)}, u32[]{:S(2)}, u32[]{:S(2)}) collective-permute-start(f32[2,64,256]{2,1,0:T(8,128)S(1)} %get-tuple-element.1083), channel_id=1, source_target_pairs={{240,0},{244,4},{248,8},{252,12},{0,16},{4,20},{8,24},{12,28},{16,... | collective-permute-start | bytes 393224 | tf_op jit(solution)/shard_map/while/body/eval_jaxpr/ppermute | solution.py:17
  392.5 11.3 %collective-permute-start.1 = (f32[2,64,256]{2,1,0:T(8,128)S(1)}, f32[2,64,256]{2,1,0:T(8,128)S(1)}, u32[]{:S(2)}, u32[]{:S(2)}) collective-permute-start(f32[2,64,256]{2,1,0:T(8,128)S(1)} %get-tuple-element.1083), channel_id=1, source_target_pairs={{240,0},{244,4},{248,8},{252,12},{0,16},{4,20},{8,24},{12,28},{16,... | collective-permute-start | bytes 393224 | tf_op jit(solution)/shard_map/while/body/eval_jaxpr/ppermute | solution.py:17
  404.8 11.9 %collective-permute-start.1 = (f32[2,64,256]{2,1,0:T(8,128)S(1)}, f32[2,64,256]{2,1,0:T(8,128)S(1)}, u32[]{:S(2)}, u32[]{:S(2)}) collective-permute-start(f32[2,64,256]{2,1,0:T(8,128)S(1)} %get-tuple-element.1083), channel_id=1, source_target_pairs={{240,0},{244,4},{248,8},{252,12},{0,16},{4,20},{8,24},{12,28},{16,... | collective-permute-start | bytes 393224 | tf_op jit(solution)/shard_map/while/body/eval_jaxpr/ppermute | solution.py:17
  417.6 12.3 %collective-permute-start.1 = (f32[2,64,256]{2,1,0:T(8,128)S(1)}, f32[2,64,256]{2,1,0:T(8,128)S(1)}, u32[]{:S(2)}, u32[]{:S(2)}) collective-permute-start(f32[2,64,256]{2,1,0:T(8,128)S(1)} %get-tuple-element.1083), channel_id=1, source_target_pairs={{240,0},{244,4},{248,8},{252,12},{0,16},{4,20},{8,24},{12,28},{16,... | collective-permute-start | bytes 393224 | tf_op jit(solution)/shard_map/while/body/eval_jaxpr/ppermute | solution.py:17
  430.8 12.5 %collective-permute-start.1 = (f32[2,64,256]{2,1,0:T(8,128)S(1)}, f32[2,64,256]{2,1,0:T(8,128)S(1)}, u32[]{:S(2)}, u32[]{:S(2)}) collective-permute-start(f32[2,64,256]{2,1,0:T(8,128)S(1)} %get-tuple-element.1083), channel_id=1, source_target_pairs={{240,0},{244,4},{248,8},{252,12},{0,16},{4,20},{8,24},{12,28},{16,... | collective-permute-start | bytes 393224 | tf_op jit(solution)/shard_map/while/body/eval_jaxpr/ppermute | solution.py:17
  444.2 12.5 %collective-permute-start.1 = (f32[2,64,256]{2,1,0:T(8,128)S(1)}, f32[2,64,256]{2,1,0:T(8,128)S(1)}, u32[]{:S(2)}, u32[]{:S(2)}) collective-permute-start(f32[2,64,256]{2,1,0:T(8,128)S(1)} %get-tuple-element.1083), channel_id=1, source_target_pairs={{240,0},{244,4},{248,8},{252,12},{0,16},{4,20},{8,24},{12,28},{16,... | collective-permute-start | bytes 393224 | tf_op jit(solution)/shard_map/while/body/eval_jaxpr/ppermute | solution.py:17
  (5 other events, 108.1 us)
where the time goes:
time: 467 us; the launch traced here: 464 us
  waiting for transfers between devices  299 us (64%)
  matrix products  41.9 us (9%)
  other arithmetic  39.9 us (9%)
  local copies, waits for them, and re-layouts  34.4 us (7%)
  loops' own time  32.9 us (7%)
  blocking collectives  5.84 us (1%)
  starting transfers between devices  5.77 us (1%)
    ppermute x30, waiting for transfers between devices, shifted(): return lax.ppermute(block, axis, route)  299 us
    another operation x1, loops' own time, per_device(): lax.map(backward_item, item_ids)  15.7 us
    another operation x1, loops' own time, per_device(): head_dots, log_totals = lax.map(forward_item, item_ids)  15.7 us
    add x15, other arithmetic, add_block(): incoming + lax.dynamic_index_in_dim(term_blocks, target, 1, keepdims=False)  13.8 us
    dot_general x8, matrix products, item_scores(): jnp.einsum('rgd,nd->grn', query_item, key_item, preferred_element_type=jn...  11.6 us
  transfers between devices with their start and end apart: 30, of which 30 were waited for; matrix products, arithmetic and copies ran while one was open for 0% of the time, Pallas kernels for 0%

commit v1 on v0

v1 whole, which is shorter than its diff:
```python
import functools
import math

import jax
import jax.numpy as jnp
from jax import lax
from jax.experimental import pallas as pl
from jax.experimental.pallas import tpu as pltpu
from jax.sharding import PartitionSpec as P

D = 128
HK = 2
NJ = 4
JR = 256
CK = 256
BK = 64
SCALE = 1.0 / math.sqrt(D)
C1 = SCALE * math.log2(math.e)
CLIP = 0.2
MESH = pl.DeviceIdType.MESH
F32 = jnp.float32
BF16 = jnp.bfloat16

OWN, UP, DOWN, FAR = 0, 1, 2, 3
RESP = 4 * CK
KEYS = RESP + 128
CHUNKS = [(0, CK), (CK, CK), (2 * CK, CK), (3 * CK, CK), (RESP, 128)]


def dot_t(a, b):
    return lax.dot_general(a, b, (((1,), (1,)), ((), ())), preferred_element_type=F32)


def dot_n(a, b):
    return jnp.dot(a, b, preferred_element_type=F32)


def kernel(
    q_hbm, rk_hbm, rv_hbm, pk_hbm, pv_hbm, ro_hbm, prox_hbm, beh_hbm, adv_hbm, len_hbm, mask_hbm,
    gq_hbm, grk_hbm, grv_hbm, gpk_hbm, gpv_hbm, loss_hbm,
    kv, kvt, qs, rs, rst, es, pb, ds, ms, ls, fs, hds, do,
    lpx, tok, tokm, adv_s, len_s, loss_s,
    y2s, y2r, y1s, y1r, joins, zs, zr, ownz,
    gq_v, gr_v, gp_v,
    ld_sem, out_sem,
    gz_s, gz_r, gy_s, gy_r, lp_s, lp_r, y2_s, y2_rs, y1_s, y1_rs, z_s, z_rs,
):
    dp = lax.axis_index("dp")
    mp = lax.axis_index("mp")
    pc = lax.axis_size("dp") // 16
    mpn = lax.axis_size("mp")
    s = lax.rem(dp, pc)
    gp = dp // pc
    y = gp // 4
    z = lax.rem(gp, 4)

    def peer(dy, dz):
        yy = lax.rem(y + dy + 4, 4)
        zz = lax.rem(z + dz + 4, 4)
        return (((yy * 4 + zz) * pc + s), mp)

    y_up, y_dn = peer(1, 0), peer(-1, 0)
    z_up, z_dn, z_far = peer(0, 1), peer(0, -1), peer(0, 2)
    mates = [(dp, lax.rem(mp + k, mpn)) for k in range(1, mpn)]

    barrier = pltpu.get_barrier_semaphore()
    friends = [y_up, y_dn, z_up, z_dn] + mates
    for f in friends:
        pl.semaphore_signal(barrier, inc=1, device_id=f, device_id_type=MESH)

    own_loads = []
    for t, src in enumerate((pk_hbm, pv_hbm)):
        for h in range(HK):
            c = pltpu.make_async_copy(
                src.at[:, h * D:(h + 1) * D], kv.at[t, h, 0:BK, :], ld_sem.at[t * HK + h]
            )
            c.start()
            own_loads.append(c)
    resp_loads = []
    for t, src in enumerate((rk_hbm, rv_hbm)):
        for h in range(HK):
            c = pltpu.make_async_copy(
                src.at[:, h * D:(h + 1) * D], kv.at[t, h, RESP:KEYS, :], ld_sem.at[4 + t * HK + h]
            )
            c.start()
            resp_loads.append(c)
    for h in range(HK):
        for t, (src, dst) in enumerate(((q_hbm, qs), (ro_hbm, rs))):
            for i in range(8):
                n = h * 8 + i
                pltpu.make_async_copy(
                    src.at[:, n * D:(n + 1) * D],
                    dst.at[h, i // 2, (i % 2) * 128:(i % 2 + 1) * 128, :],
                    ld_sem.at[8 + t * HK + h],
                ).start()
    small = [
        pltpu.make_async_copy(prox_hbm, tok.at[0], ld_sem.at[12]),
        pltpu.make_async_copy(beh_hbm, tok.at[1], ld_sem.at[13]),
        pltpu.make_async_copy(mask_hbm, tokm, ld_sem.at[14]),
        pltpu.make_async_copy(adv_hbm, adv_s, ld_sem.at[15]),
        pltpu.make_async_copy(len_hbm, len_s, ld_sem.at[16]),
    ]
    for c in small:
        c.start()

    def wait_rows(h):
        for t, dst in enumerate((qs, rs)):
            pltpu.make_async_copy(dst.at[h], dst.at[h], ld_sem.at[8 + t * HK + h]).wait()

    def turn_rows(h):
        for j in range(NJ):
            rst[h, j] = rs[h, j].T

    sends = []

    def send(src, dst, ss, rsem, to):
        c = pltpu.make_async_remote_copy(
            src_ref=src, dst_ref=dst, send_sem=ss, recv_sem=rsem, device_id=to, device_id_type=MESH
        )
        c.start()
        sends.append(c)

    def arrived(dst, rsem):
        pltpu.make_async_remote_copy(
            src_ref=dst, dst_ref=dst, send_sem=rsem, recv_sem=rsem, device_id=y_up, device_id_type=MESH
        ).wait_recv()

    def kvb(t, h, dz, dy):
        lo = dz * CK + dy * BK
        tt = slice(0, 2) if t is None else slice(t, t + 1)
        return kv.at[tt, h, lo:lo + BK, :]

    def z_own():
        for t in range(2):
            for h in range(HK):
                send(kvb(1 - t, h, OWN, OWN), kvb(1 - t, h, DOWN, OWN),
                     gz_s.at[h, 1 - t, 0], gz_r.at[h, 1 - t, 0], z_up)
                send(kvb(t, h, OWN, OWN), kvb(t, h, UP, OWN),
                     gz_s.at[h, t, 1], gz_r.at[h, t, 1], z_dn)

    def z_forward(h):
        arrived(kvb(1, h, DOWN, OWN), gz_r.at[h, 1, 0])
        send(kvb(1, h, DOWN, OWN), kvb(1, h, FAR, OWN), gz_s.at[h, 1, 2], gz_r.at[h, 1, 2], z_up)
        arrived(kvb(0, h, UP, OWN), gz_r.at[h, 0, 1])
        send(kvb(0, h, UP, OWN), kvb(0, h, FAR, OWN), gz_s.at[h, 0, 2], gz_r.at[h, 0, 2], z_dn)

    def z_rest(h):
        arrived(kvb(0, h, DOWN, OWN), gz_r.at[h, 0, 0])
        arrived(kvb(1, h, UP, OWN), gz_r.at[h, 1, 1])

    def z_last(h):
        arrived(kvb(1, h, FAR, OWN), gz_r.at[h, 1, 2])
        arrived(kvb(0, h, FAR, OWN), gz_r.at[h, 0, 2])

    def y_send(h, dz):
        send(kvb(None, h, dz, OWN), kvb(None, h, dz, DOWN),
             gy_s.at[h, dz, 0], gy_r.at[h, dz, 0], y_up)
        send(kvb(None, h, dz, OWN), kvb(None, h, dz, UP),
             gy_s.at[h, dz, 1], gy_r.at[h, dz, 1], y_dn)

    def y_forward(h, dz):
        arrived(kvb(None, h, dz, DOWN), gy_r.at[h, dz, 0])
        send(kvb(1, h, dz, DOWN), kvb(1, h, dz, FAR),
             gy_s.at[h, dz, 2], gy_r.at[h, dz, 2], y_up)
        arrived(kvb(None, h, dz, UP), gy_r.at[h, dz, 1])
        send(kvb(0, h, dz, UP), kvb(0, h, dz, FAR),
             gy_s.at[h, dz, 3], gy_r.at[h, dz, 3], y_dn)

    def y_last(h, dz):
        arrived(kvb(1, h, dz, FAR), gy_r.at[h, dz, 2])
        arrived(kvb(0, h, dz, FAR), gy_r.at[h, dz, 3])

    def fwd(h, ci):
        off, nk = CHUNKS[ci]

        def body(j, _):
            sc = dot_t(kv[0, h, off:off + nk, :], qs[h, j])
            if ci == 4:
                key = lax.broadcasted_iota(jnp.int32, (nk, JR), 0)
                row = lax.broadcasted_iota(jnp.int32, (nk, JR), 1)
                sc = jnp.where(key <= lax.rem(row, 128), sc, -jnp.inf)
            m = jnp.max(sc, axis=0, keepdims=True) * C1
            e = jnp.exp2(sc * C1 - m)
            es[h, j, off:off + nk, :] = e
            ms[h, j, ci:ci + 1, :] = m
            ls[h, j, ci:ci + 1, :] = jnp.sum(e, axis=0, keepdims=True)
            return 0

        for t in range(2):
            kvt[t, h, :, off:off + nk] = kv[t, h, off:off + nk, :].T
        lax.fori_loop(0, NJ, body, 0, unroll=True)

    def normalise(h, lp):
        def body(j, lp):
            mc = ms[h, j, 0:5, :]
            m = jnp.max(mc, axis=0, keepdims=True)
            f = jnp.exp2(mc - m)
            total = jnp.sum(f * ls[h, j, 0:5, :], axis=0, keepdims=True)
            f = f / total
            fs[h, j, 0:5, :] = f
            for ci, (off, nk) in enumerate(CHUNKS):
                p = (es[h, j, off:off + nk, :] * f[ci:ci + 1, :]).astype(BF16)
                pb[h, j, off:off + nk, :] = p
            attended = dot_n(kvt[1, h], pb[h, j])
            hd = jnp.sum(attended * rst[h, j].astype(F32), axis=0, keepdims=True)
            hds[h, j, 0:1, :] = hd
            return lp + hd[:, :128] + hd[:, 128:]

        return lax.fori_loop(0, NJ, body, lp, unroll=True)

    for c in own_loads:
        c.wait()
    pl.semaphore_wait(barrier, len(friends))
    z_own()
    for h in range(HK):
        y_send(h, OWN)
    for c in resp_loads:
        c.wait()
    wait_rows(0)
    fwd(0, 4)
    for h in range(HK):
        y_forward(h, OWN)
        z_forward(h)
    for h in range(HK):
        z_rest(h)
        y_send(h, UP)
        y_send(h, DOWN)
    wait_rows(1)
    turn_rows(0)
    for h in range(HK):
        z_last(h)
        y_send(h, FAR)
    y_last(0, OWN)
    fwd(0, OWN)
    for h in range(HK):
        y_forward(h, UP)
        y_forward(h, DOWN)
    y_last(1, OWN)
    fwd(1, OWN)
    for h in range(HK):
        y_forward(h, FAR)
    fwd(1, 4)
    turn_rows(1)
    for h in range(HK):
        for dz in (UP, DOWN):
            y_last(h, dz)
            fwd(h, dz)
    lp = jnp.zeros((1, 128), F32)
    for h in range(HK):
        y_last(h, FAR)
        fwd(h, FAR)
        lp = normalise(h, lp)

    lpx[mp] = jnp.broadcast_to(lp, (8, 128))
    for k, mate in enumerate(mates):
        send(lpx.at[mp], lpx.at[mp], lp_s.at[k], lp_r.at[k], mate)
    for c in small:
        c.wait()
    for k in range(mpn - 1):
        src = lax.rem(mp + mpn - 1 - k, mpn)
        arrived(lpx.at[src], lp_r.at[k])
    log_prob = jnp.zeros((1, 128), F32)
    for k in range(mpn):
        log_prob = log_prob + lpx[k, 0:1, :]
    prox = tok[0]
    adv = adv_s[0]
    length = len_s[0]
    ratio = jnp.exp(log_prob - prox)
    importance = jnp.exp(prox - tok[1])
    squashed = jnp.tanh((ratio - 1.0) / CLIP)
    clipped = 1.0 + CLIP * squashed
    token = lax.broadcasted_iota(jnp.int32, (1, 128), 1)
    valid = (token < length) & (tokm[...] == 1)
    lens = jnp.broadcast_to(length, (1, 128)).astype(F32)
    token_scale = jnp.where(valid, 128.0 / lens, 0.0)
    objective = jnp.minimum(ratio * adv, clipped * adv)
    loss_s[0] = -jnp.sum(token_scale * importance * objective)
    slope = jnp.where(adv * (ratio - 1.0) > 0, 1.0 - squashed * squashed, 1.0)
    g = -token_scale * importance * adv * ratio * slope
    loss_out = pltpu.make_async_copy(loss_s, loss_hbm, out_sem.at[0])
    loss_out.start()
    g_rows = jnp.concatenate([g, g], axis=1)
    g_cols = jnp.broadcast_to(g, (128, 128)).T
    g_cols = jnp.concatenate([g_cols, g_cols], axis=0)

    def grad_out(h):
        def body(j, _):
            do[h, j] = (g_cols * rs[h, j].astype(F32)).astype(BF16)
            return 0

        lax.fori_loop(0, NJ, body, 0, unroll=True)

    def value_grad(h, ci):
        off, nk = CHUNKS[ci]
        acc = dot_n(pb[h, 0, off:off + nk, :], do[h, 0])
        for j in range(1, NJ):
            acc = acc + dot_n(pb[h, j, off:off + nk, :], do[h, j])
        return acc

    def key_grad(h, ci):
        off, nk = CHUNKS[ci]
        acc = None
        for j in range(NJ):
            grad_probs = dot_t(kv[1, h, off:off + nk, :], do[h, j])
            d = (es[h, j, off:off + nk, :] * fs[h, j, ci:ci + 1, :]) * (
                grad_probs - hds[h, j, 0:1, :] * g_rows
            )
            d = d.astype(BF16)
            ds[h, j, off:off + nk, :] = d
            part = dot_n(d, qs[h, j])
            acc = part if acc is None else acc + part
        return acc * SCALE

    def rows_of(dy):
        return slice(dy * BK, (dy + 1) * BK)

    def terms(dz, h):
        v = value_grad(h, dz)
        y2s[0, dz, h] = v[rows_of(FAR)].astype(BF16)
        y1s[1, 0, dz, h] = v[rows_of(DOWN)].astype(BF16)
        joins[0, dz, h] = v[rows_of(UP)]
        ownz[0, dz, h] = v[rows_of(OWN)]
        k = key_grad(h, dz)
        y2s[1, dz, h] = k[rows_of(FAR)].astype(BF16)
        y1s[0, 1, dz, h] = k[rows_of(UP)].astype(BF16)
        joins[1, dz, h] = k[rows_of(DOWN)]
        ownz[1, dz, h] = k[rows_of(OWN)]

    def y1_send(way, t, dz, h):
        send(y1s.at[way, t, dz, h], y1r.at[way, t, dz, h],
             y1_s.at[way, t, dz, h], y1_rs.at[way, t, dz, h], y_up if way == 0 else y_dn)

    def first_sends(dz, h):
        for t, to in enumerate((y_up, y_dn)):
            send(y2s.at[t, dz, h], y2r.at[t, dz, h],
                 y2_s.at[t, dz, h], y2_rs.at[t, dz, h], to)
        y1_send(0, 1, dz, h)
        y1_send(1, 0, dz, h)

    def join_sends(dz, h):
        for t in range(2):
            arrived(y2r.at[t, dz, h], y2_rs.at[t, dz, h])
            y1s[t, t, dz, h] = (joins[t, dz, h] + y2r[t, dz, h].astype(F32)).astype(BF16)
            y1_send(t, t, dz, h)

    def y_total(dz, h):
        for t in range(2):
            for way in range(2):
                arrived(y1r.at[way, t, dz, h], y1_rs.at[way, t, dz, h])
            total = ownz[t, dz, h] + (
                y1r[0, t, dz, h].astype(F32) + y1r[1, t, dz, h].astype(F32)
            )
            if dz == OWN:
                ownz[t, dz, h] = total
            else:
                zs[dz - 1, h, t] = total.astype(BF16)
        if dz != OWN:
            send(zs.at[dz - 1, h], zr.at[dz - 1, h], z_s.at[dz - 1, h], z_rs.at[dz - 1, h],
                 (z_up, z_dn, z_far)[dz - 1])

    GROUPS = ((FAR, 0), (FAR, 1), (UP, 0), (DOWN, 0), (UP, 1), (DOWN, 1), (OWN, 0), (OWN, 1))
    for h in range(HK):
        grad_out(h)
    for n, group in enumerate(GROUPS):
        terms(*group)
        first_sends(*group)
        if n >= 2:
            join_sends(*GROUPS[n - 2])
        if n >= 4:
            y_total(*GROUPS[n - 4])

    outs = []

    def put(src, dst, n):
        c = pltpu.make_async_copy(src, dst, out_sem.at[n])
        c.start()
        outs.append(c)

    for n in (6, 7):
        join_sends(*GROUPS[n])
    y_total(*GROUPS[4])
    for h in range(HK):
        gr_v[0, :, h * D:(h + 1) * D] = key_grad(h, 4).astype(BF16)
        gr_v[1, :, h * D:(h + 1) * D] = value_grad(h, 4).astype(BF16)
    put(gr_v.at[0], grk_hbm, 1)
    put(gr_v.at[1], grv_hbm, 2)

    def query_grad(h):
        def body(j, _):
            gq_v[h, j] = (dot_n(kvt[0, h], ds[h, j]) * SCALE).T.astype(BF16)
            return 0

        lax.fori_loop(0, NJ, body, 0, unroll=True)
        for i in range(8):
            n = h * 8 + i
            put(gq_v.at[h, i // 2, (i % 2) * 128:(i % 2 + 1) * 128, :],
                gq_hbm.at[:, n * D:(n + 1) * D], 5 + n)

    y_total(*GROUPS[5])
    query_grad(0)
    query_grad(1)
    for h in range(HK):
        y_total(OWN, h)
    for h in range(HK):
        for b in (2, 0, 1):
            arrived(zr.at[b, h], z_rs.at[b, h])
        for t in range(2):
            total = ownz[t, OWN, h]
            for b in range(3):
                total = total + zr[b, h, t].astype(F32)
            gp_v[t, :, h * D:(h + 1) * D] = total.astype(BF16)
    put(gp_v.at[1], gpk_hbm, 3)
    put(gp_v.at[0], gpv_hbm, 4)
    loss_out.wait()
    for c in outs:
        c.wait()
    for c in sends:
        c.wait_send()


def hand_over(*refs):
    held, sem = refs[12:18], refs[18]
    loads = [pltpu.make_async_copy(refs[n], held[n], sem.at[0, n]) for n in range(6)]
    stores = [pltpu.make_async_copy(held[n], refs[6 + n], sem.at[1, n]) for n in range(6)]
    for c in loads:
        c.start()
    for n in range(6):
        loads[n].wait()
        stores[n].start()
    for c in stores:
        c.wait()


def per_device(q, rk, rv, pk, pv, ro, prox, beh, adv, lens, mask):
    rows = q.shape[0]
    any_spec = pl.BlockSpec(memory_space=pl.ANY)
    dma = pltpu.SemaphoreType.DMA
    vm = pltpu.VMEM
    mpn = lax.axis_size("mp")
    outs = pl.pallas_call(
        kernel,
        out_shape=(
            jax.ShapeDtypeStruct(q.shape, BF16),
            jax.ShapeDtypeStruct(rk.shape, BF16),
            jax.ShapeDtypeStruct(rv.shape, BF16),
            jax.ShapeDtypeStruct(pk.shape, BF16),
            jax.ShapeDtypeStruct(pv.shape, BF16),
            jax.ShapeDtypeStruct((1,), F32),
        ),
        in_specs=[any_spec] * 11,
        out_specs=(any_spec,) * 6,
        scratch_shapes=[
            vm((2, HK, KEYS, D), BF16),
            vm((2, HK, D, KEYS), BF16),
            vm((HK, NJ, JR, D), BF16),
            vm((HK, NJ, JR, D), BF16),
            vm((HK, NJ, D, JR), BF16),
            vm((HK, NJ, KEYS, JR), F32),
            vm((HK, NJ, KEYS, JR), BF16),
            vm((HK, NJ, KEYS, JR), BF16),
            vm((HK, NJ, 8, JR), F32),
            vm((HK, NJ, 8, JR), F32),
            vm((HK, NJ, 8, JR), F32),
            vm((HK, NJ, 8, JR), F32),
            vm((HK, NJ, JR, D), BF16),
            vm((mpn, 8, 128), F32),
            vm((2, 1, 128), F32),
            vm((1, 128), jnp.int32),
            pltpu.SMEM((1,), F32),
            pltpu.SMEM((1,), jnp.int32),
            pltpu.SMEM((1,), F32),
            vm((2, 4, HK, BK, D), BF16),
            vm((2, 4, HK, BK, D), BF16),
            vm((2, 2, 4, HK, BK, D), BF16),
            vm((2, 2, 4, HK, BK, D), BF16),
            vm((2, 4, HK, BK, D), F32),
            vm((3, HK, 2, BK, D), BF16),
            vm((3, HK, 2, BK, D), BF16),
            vm((2, 4, HK, BK, D), F32),
            vm((HK, NJ, JR, D), BF16),
            vm((2, rows, HK * D), BF16),
            vm((2, BK, HK * D), BF16),
            dma((17,)),
            dma((21,)),
            dma((HK, 2, 3)),
            dma((HK, 2, 3)),
            dma((HK, 4, 4)),
            dma((HK, 4, 4)),
            dma((max(mpn - 1, 1),)),
            dma((max(mpn - 1, 1),)),
            dma((2, 4, HK)),
            dma((2, 4, HK)),
            dma((2, 2, 4, HK)),
            dma((2, 2, 4, HK)),
            dma((3, HK)),
            dma((3, HK)),
        ],
        compiler_params=pltpu.CompilerParams(
            collective_id=0, has_side_effects=True, vmem_limit_bytes=63 * 1024 * 1024
        ),
        name="attention_gradient",
    )(q, rk, rv, pk, pv, ro, prox.reshape(1, rows), beh.reshape(1, rows), adv, lens,
      mask.reshape(1, rows))
    return pl.pallas_call(
        hand_over,
        out_shape=tuple(jax.ShapeDtypeStruct(o.shape, o.dtype) for o in outs),
        in_specs=[any_spec] * 6,
        out_specs=(any_spec,) * 6,
        scratch_shapes=[vm(o.shape, o.dtype) for o in outs[:5]]
        + [pltpu.SMEM((1,), F32), dma((2, 6))],
        compiler_params=pltpu.CompilerParams(vmem_limit_bytes=63 * 1024 * 1024),
        name="hand_over",
    )(*outs)


def solution(mesh):
    wide = P("dp", "mp")
    row = P("dp")
    return jax.shard_map(
        per_device,
        mesh=mesh,
        in_specs=(wide,) * 6 + (row,) * 5,
        out_specs=(wide,) * 5 + (row,),
        check_vma=False,
    )
```

time: 467 us -> 53.5 us (0.11)
  waiting for transfers between devices: 299 us -> 0 us
  Pallas kernels: 0 us -> 51.4 us
  matrix products: 41.9 us -> 0 us
  other arithmetic: 39.9 us -> 0 us
  local copies, waits for them, and re-layouts: 34.4 us -> 0 us
  loops' own time: 32.9 us -> 0 us
  blocking collectives: 5.84 us -> 0 us
  starting transfers between devices: 5.77 us -> 0 us
    ppermute x30 -> x0, waiting for transfers between devices: 299 us -> none  [shifted(): return lax.ppermute(block, axis, route)]
    pallas_call x0 -> x2, Pallas kernels: none -> 51.4 us  [the longest x1 48.7 us: per_device(): pl.pallas_call(kernel, out_shape=(jax.ShapeDtypeStruct(q.shape, BF16), ja...]
    dot_general x28 -> x0, matrix products: 41.9 us -> none  [the longest x8 11.6 us: item_scores(): jnp.einsum('rgd,nd->grn', query_item, key_item, preferred_element_type=jn...]
    another operation x4 -> x0, loops' own time: 32.9 us -> none  [the longest x1 15.7 us: per_device(): lax.map(backward_item, item_ids)]
    add x15 -> x0, other arithmetic: 13.8 us -> none  [add_block(): incoming + lax.dynamic_index_in_dim(term_blocks, target, 1, keepdims=False)]
    dynamic_slice x16 -> x0, local copies, waits for them, and re-layouts: 8.84 us -> none  [the longest x8 4.66 us: per_device(): head_dots, log_totals = lax.map(forward_item, item_ids)]
    unnamed x25 -> x0, local copies, waits for them, and re-layouts: 8.01 us -> none
    or x8 -> x0, other arithmetic: 6.91 us -> none  [allowed_mask(): return (key_ids < prompt_len) | (key_ids - prompt_len <= query_ids)]
  transfers between devices with their start and end apart: 30 -> 0, of which waited for: 30 -> 0; matrix products, arithmetic and copies ran while one was open for 0% -> 0% of each run, Pallas kernels for 0% -> 0%
where the time goes in v1:
time: 53.5 us; the launch traced here: 53.3 us
  Pallas kernels  51.4 us (96%)
  between operations  1.93 us (4%)
    pallas_call x1, Pallas kernels, per_device(): pl.pallas_call(kernel, out_shape=(jax.ShapeDtypeStruct(q.shape, BF16), ja...  48.7 us
    pallas_call x1, Pallas kernels, per_device(): pl.pallas_call(hand_over, out_shape=tuple((jax.ShapeDtypeStruct(o.shape,...  2.61 us

profile of v1, /device:TPU:4, one launch (start us, length us, event | category | flops | bytes accessed | tf_op | source)
XLA Modules:
  0.0 53.3 jit_solution(7180455808643541219)
XLA Ops:
  1.9 48.7 %attention_gradient.1 = (bf16[128,2048]{1,0:T(8,128)(2,1)}, bf16[128,256]{1,0:T(8,128)(2,1)}, bf16[128,256]{1,0:T(8,128)(2,1)}, bf16[64,256]{1,0:T(8,128)(2,1)}, bf16[64,256]{1,0:T(8,128)(2,1)}, /*index=5*/f32[1]{0:T(128)}) custom-call(bf16[128,2048]{1,0:T(8,128)(2,1)} %q_hbm.1, bf16[128,256]{1,0:T(8,128)(2,1)} %rk_hbm.1, bf16[128,256]{1,0:T(8,128)(2,1)} %rv_hbm.1, ...), custom_call_target="tpu_custom_call" | custom-call | tf_op jit(solution)/shard_map/attention_gradient/pallas_call | solution.py:440
  50.7 2.6 %hand_over.1 = (bf16[128,2048]{1,0:T(8,128)(2,1)}, bf16[128,256]{1,0:T(8,128)(2,1)}, bf16[128,256]{1,0:T(8,128)(2,1)}, bf16[64,256]{1,0:T(8,128)(2,1)}, bf16[64,256]{1,0:T(8,128)(2,1)}, /*index=5*/f32[1]{0:T(128)}) custom-call(bf16[128,2048]{1,0:T(8,128)(2,1)} %get-tuple-element.12.refs_0_, bf16[128,256]{1,0:T(8,128)(2,1)} %get-tuple-element.13.refs_1_, ...), custom_call_target="tpu_custom_call" | custom-call | tf_op jit(solution)/shard_map/hand_over/pallas_call | solution.py:504

commit v2 on v1

--- a/solution.py
+++ b/solution.py
@@ -37,11 +37,10 @@
 
 def kernel(
     q_hbm, rk_hbm, rv_hbm, pk_hbm, pv_hbm, ro_hbm, prox_hbm, beh_hbm, adv_hbm, len_hbm, mask_hbm,
-    gq_hbm, grk_hbm, grv_hbm, gpk_hbm, gpv_hbm, loss_hbm,
-    kv, kvt, qs, rs, rst, es, pb, ds, ms, ls, fs, hds, do,
+    gq_out, grk_out, grv_out, gpk_out, gpv_out, loss_hbm,
+    kv, kvt, qs, rs, rst, es, att, pb, ds, ms, ls, fs, hds, do,
     lpx, tok, tokm, adv_s, len_s, loss_s,
     y2s, y2r, y1s, y1r, joins, zs, zr, ownz,
-    gq_v, gr_v, gp_v,
     ld_sem, out_sem,
     gz_s, gz_r, gy_s, gy_r, lp_s, lp_r, y2_s, y2_rs, y1_s, y1_rs, z_s, z_rs,
 ):
@@ -59,12 +58,12 @@
         zz = lax.rem(z + dz + 4, 4)
         return (((yy * 4 + zz) * pc + s), mp)
 
-    y_up, y_dn = peer(1, 0), peer(-1, 0)
+    y_up, y_dn, y_far = peer(1, 0), peer(-1, 0), peer(2, 0)
     z_up, z_dn, z_far = peer(0, 1), peer(0, -1), peer(0, 2)
     mates = [(dp, lax.rem(mp + k, mpn)) for k in range(1, mpn)]
 
     barrier = pltpu.get_barrier_semaphore()
-    friends = [y_up, y_dn, z_up, z_dn] + mates
+    friends = [y_up, y_dn, y_far, z_up, z_dn] + mates
     for f in friends:
         pl.semaphore_signal(barrier, inc=1, device_id=f, device_id_type=MESH)
 
@@ -127,48 +126,49 @@
 
     def kvb(t, h, dz, dy):
         lo = dz * CK + dy * BK
-        tt = slice(0, 2) if t is None else slice(t, t + 1)
-        return kv.at[tt, h, lo:lo + BK, :]
-
-    def z_own():
-        for t in range(2):
-            for h in range(HK):
-                send(kvb(1 - t, h, OWN, OWN), kvb(1 - t, h, DOWN, OWN),
-                     gz_s.at[h, 1 - t, 0], gz_r.at[h, 1 - t, 0], z_up)
-                send(kvb(t, h, OWN, OWN), kvb(t, h, UP, OWN),
-                     gz_s.at[h, t, 1], gz_r.at[h, t, 1], z_dn)
-
-    def z_forward(h):
-        arrived(kvb(1, h, DOWN, OWN), gz_r.at[h, 1, 0])
-        send(kvb(1, h, DOWN, OWN), kvb(1, h, FAR, OWN), gz_s.at[h, 1, 2], gz_r.at[h, 1, 2], z_up)
-        arrived(kvb(0, h, UP, OWN), gz_r.at[h, 0, 1])
-        send(kvb(0, h, UP, OWN), kvb(0, h, FAR, OWN), gz_s.at[h, 0, 2], gz_r.at[h, 0, 2], z_dn)
-
-    def z_rest(h):
-        arrived(kvb(0, h, DOWN, OWN), gz_r.at[h, 0, 0])
-        arrived(kvb(1, h, UP, OWN), gz_r.at[h, 1, 1])
-
-    def z_last(h):
-        arrived(kvb(1, h, FAR, OWN), gz_r.at[h, 1, 2])
-        arrived(kvb(0, h, FAR, OWN), gz_r.at[h, 0, 2])
-
-    def y_send(h, dz):
-        send(kvb(None, h, dz, OWN), kvb(None, h, dz, DOWN),
-             gy_s.at[h, dz, 0], gy_r.at[h, dz, 0], y_up)
-        send(kvb(None, h, dz, OWN), kvb(None, h, dz, UP),
-             gy_s.at[h, dz, 1], gy_r.at[h, dz, 1], y_dn)
-
-    def y_forward(h, dz):
-        arrived(kvb(None, h, dz, DOWN), gy_r.at[h, dz, 0])
-        send(kvb(1, h, dz, DOWN), kvb(1, h, dz, FAR),
-             gy_s.at[h, dz, 2], gy_r.at[h, dz, 2], y_up)
-        arrived(kvb(None, h, dz, UP), gy_r.at[h, dz, 1])
-        send(kvb(0, h, dz, UP), kvb(0, h, dz, FAR),
-             gy_s.at[h, dz, 3], gy_r.at[h, dz, 3], y_dn)
-
-    def y_last(h, dz):
-        arrived(kvb(1, h, dz, FAR), gy_r.at[h, dz, 2])
-        arrived(kvb(0, h, dz, FAR), gy_r.at[h, dz, 3])
+        return kv.at[t, h, lo:lo + BK, :]
+
+    def move(t, h, a, b, ss, rsem, to):
+        send(kvb(t, h, *a), kvb(t, h, *b), ss, rsem, to)
+
+    def z_piece(t, h, way):
+        move(t, h, (OWN, OWN), ((DOWN, UP)[way], OWN),
+             gz_s.at[t, h, way], gz_r.at[t, h, way], (z_up, z_dn)[way])
+
+    def z_pass(t, h):
+        dz, n, to = (UP, 1, z_dn) if t == 0 else (DOWN, 0, z_up)
+        arrived(kvb(t, h, dz, OWN), gz_r.at[t, h, n])
+        move(t, h, (dz, OWN), (FAR, OWN), gz_s.at[t, h, 2], gz_r.at[t, h, 2], to)
+        y_send(t, h, dz)
+
+    def z_other(t, h):
+        dz, n = (DOWN, 0) if t == 0 else (UP, 1)
+        arrived(kvb(t, h, dz, OWN), gz_r.at[t, h, n])
+        y_send(t, h, dz)
+
+    def z_last(t, h):
+        arrived(kvb(t, h, FAR, OWN), gz_r.at[t, h, 2])
+        y_send(t, h, FAR)
+
+    def y_send(t, h, dz):
+        if dz in (OWN, FAR):
+            move(t, h, (dz, OWN), (dz, FAR), gy_s.at[t, h, dz, 2], gy_r.at[t, h, dz, 2], y_far)
+        move(t, h, (dz, OWN), (dz, DOWN), gy_s.at[t, h, dz, 0], gy_r.at[t, h, dz, 0], y_up)
+        move(t, h, (dz, OWN), (dz, UP), gy_s.at[t, h, dz, 1], gy_r.at[t, h, dz, 1], y_dn)
+
+    def z_fill(t, h):
+        arrived(kvb(t, h, OWN, FAR), gy_r.at[t, h, OWN, 2])
+        move(t, h, (OWN, FAR), (DOWN, FAR), gz_s.at[t, h, 3], gz_r.at[t, h, 3], z_up)
+        move(t, h, (OWN, FAR), (UP, FAR), gz_s.at[t, h, 4], gz_r.at[t, h, 4], z_dn)
+
+    def y_last(t, h, dz):
+        arrived(kvb(t, h, dz, DOWN), gy_r.at[t, h, dz, 0])
+        arrived(kvb(t, h, dz, UP), gy_r.at[t, h, dz, 1])
+        if dz == FAR:
+            arrived(kvb(t, h, dz, FAR), gy_r.at[t, h, dz, 2])
+        elif dz != OWN:
+            n = 3 if dz == DOWN else 4
+            arrived(kvb(t, h, dz, FAR), gz_r.at[t, h, n])
 
     def fwd(h, ci):
         off, nk = CHUNKS[ci]
@@ -186,12 +186,14 @@
             ls[h, j, ci:ci + 1, :] = jnp.sum(e, axis=0, keepdims=True)
             return 0
 
-        for t in range(2):
-            kvt[t, h, :, off:off + nk] = kv[t, h, off:off + nk, :].T
         lax.fori_loop(0, NJ, body, 0, unroll=True)
 
-    def normalise(h, lp):
-        def body(j, lp):
+    def turn_keys(t, h, ci):
+        off, nk = CHUNKS[ci]
+        kvt[t, h, :, off:off + nk] = kv[t, h, off:off + nk, :].T
+
+    def normalise(h):
+        for j in range(NJ):
             mc = ms[h, j, 0:5, :]
             m = jnp.max(mc, axis=0, keepdims=True)
             f = jnp.exp2(mc - m)
@@ -199,57 +201,78 @@
             f = f / total
             fs[h, j, 0:5, :] = f
             for ci, (off, nk) in enumerate(CHUNKS):
-                p = (es[h, j, off:off + nk, :] * f[ci:ci + 1, :]).astype(BF16)
-                pb[h, j, off:off + nk, :] = p
-            attended = dot_n(kvt[1, h], pb[h, j])
+                pb[h, j, off:off + nk, :] = (
+                    es[h, j, off:off + nk, :] * f[ci:ci + 1, :]
+                ).astype(BF16)
+
+    def attend(h):
+        for dz in (OWN, UP, DOWN, 4):
+            turn_keys(1, h, dz)
+        for j in range(NJ):
+            att[h, j] = dot_n(kvt[1, h, :, 0:3 * CK], pb[h, j, 0:3 * CK, :]) + dot_n(
+                kvt[1, h, :, RESP:KEYS], pb[h, j, RESP:KEYS, :]
+            )
+
+    def attend_last(h, lp):
+        turn_keys(1, h, FAR)
+        for j in range(NJ):
+            attended = att[h, j] + dot_n(kvt[1, h, :, 3 * CK:RESP], pb[h, j, 3 * CK:RESP, :])
             hd = jnp.sum(attended * rst[h, j].astype(F32), axis=0, keepdims=True)
             hds[h, j, 0:1, :] = hd
-            return lp + hd[:, :128] + hd[:, 128:]
-
-        return lax.fori_loop(0, NJ, body, lp, unroll=True)
+            lp = lp + hd[:, :128] + hd[:, 128:]
+        return lp
 
     for c in own_loads:
         c.wait()
     pl.semaphore_wait(barrier, len(friends))
-    z_own()
-    for h in range(HK):
-        y_send(h, OWN)
+    heads = range(HK)
+    for t in range(2):
+        for h in heads:
+            for way in range(2):
+                z_piece(t if way else 1 - t, h, way)
+    for t in range(2):
+        for h in heads:
+            y_send(t, h, OWN)
     for c in resp_loads:
         c.wait()
     wait_rows(0)
     fwd(0, 4)
-    for h in range(HK):
-        y_forward(h, OWN)
-        z_forward(h)
-    for h in range(HK):
-        z_rest(h)
-        y_send(h, UP)
-        y_send(h, DOWN)
+    for h in heads:
+        z_pass(0, h)
+        z_pass(1, h)
+    for t in range(2):
+        for h in heads:
+            z_other(t, h)
+    for h in heads:
+        z_fill(0, h)
     wait_rows(1)
-    turn_rows(0)
-    for h in range(HK):
-        z_last(h)
-        y_send(h, FAR)
-    y_last(0, OWN)
-    fwd(0, OWN)
-    for h in range(HK):
-        y_forward(h, UP)
-        y_forward(h, DOWN)
-    y_last(1, OWN)
-    fwd(1, OWN)
-    for h in range(HK):
-        y_forward(h, FAR)
     fwd(1, 4)
-    turn_rows(1)
-    for h in range(HK):
+    for h in heads:
+        z_last(0, h)
+    for h in heads:
+        z_fill(1, h)
+    for h in heads:
+        z_last(1, h)
+    for h in heads:
+        turn_rows(h)
+        y_last(0, h, OWN)
+        fwd(h, OWN)
+    for h in heads:
         for dz in (UP, DOWN):
-            y_last(h, dz)
+            y_last(0, h, dz)
             fwd(h, dz)
+    for h in heads:
+        y_last(0, h, FAR)
+        fwd(h, FAR)
+        normalise(h)
+    for h in heads:
+        for dz in (OWN, UP, DOWN):
+            y_last(1, h, dz)
+        attend(h)
     lp = jnp.zeros((1, 128), F32)
-    for h in range(HK):
-        y_last(h, FAR)
-        fwd(h, FAR)
-        lp = normalise(h, lp)
+    for h in heads:
+        y_last(1, h, FAR)
+        lp = attend_last(h, lp)
 
     lpx[mp] = jnp.broadcast_to(lp, (8, 128))
     for k, mate in enumerate(mates):
@@ -273,12 +296,8 @@
     valid = (token < length) & (tokm[...] == 1)
     lens = jnp.broadcast_to(length, (1, 128)).astype(F32)
     token_scale = jnp.where(valid, 128.0 / lens, 0.0)
-    objective = jnp.minimum(ratio * adv, clipped * adv)
-    loss_s[0] = -jnp.sum(token_scale * importance * objective)
     slope = jnp.where(adv * (ratio - 1.0) > 0, 1.0 - squashed * squashed, 1.0)
     g = -token_scale * importance * adv * ratio * slope
-    loss_out = pltpu.make_async_copy(loss_s, loss_hbm, out_sem.at[0])
-    loss_out.start()
     g_rows = jnp.concatenate([g, g], axis=1)
     g_cols = jnp.broadcast_to(g, (128, 128)).T
     g_cols = jnp.concatenate([g_cols, g_cols], axis=0)
@@ -318,11 +337,13 @@
         v = value_grad(h, dz)
         y2s[0, dz, h] = v[rows_of(FAR)].astype(BF16)
         y1s[1, 0, dz, h] = v[rows_of(DOWN)].astype(BF16)
+        first_sends(0, dz, h)
         joins[0, dz, h] = v[rows_of(UP)]
         ownz[0, dz, h] = v[rows_of(OWN)]
         k = key_grad(h, dz)
         y2s[1, dz, h] = k[rows_of(FAR)].astype(BF16)
         y1s[0, 1, dz, h] = k[rows_of(UP)].astype(BF16)
+        first_sends(1, dz, h)
         joins[1, dz, h] = k[rows_of(DOWN)]
         ownz[1, dz, h] = k[rows_of(OWN)]
 
@@ -330,12 +351,10 @@
         send(y1s.at[way, t, dz, h], y1r.at[way, t, dz, h],
              y1_s.at[way, t, dz, h], y1_rs.at[way, t, dz, h], y_up if way == 0 else y_dn)
 
-    def first_sends(dz, h):
-        for t, to in enumerate((y_up, y_dn)):
-            send(y2s.at[t, dz, h], y2r.at[t, dz, h],
-                 y2_s.at[t, dz, h], y2_rs.at[t, dz, h], to)
-        y1_send(0, 1, dz, h)
-        y1_send(1, 0, dz, h)
+    def first_sends(t, dz, h):
+        send(y2s.at[t, dz, h], y2r.at[t, dz, h],
+             y2_s.at[t, dz, h], y2_rs.at[t, dz, h], (y_up, y_dn)[t])
+        y1_send(1 - t, t, dz, h)
 
     def join_sends(dz, h):
         for t in range(2):
@@ -359,46 +378,38 @@
                  (z_up, z_dn, z_far)[dz - 1])
 
     GROUPS = ((FAR, 0), (FAR, 1), (UP, 0), (DOWN, 0), (UP, 1), (DOWN, 1), (OWN, 0), (OWN, 1))
-    for h in range(HK):
-        grad_out(h)
     for n, group in enumerate(GROUPS):
+        if n < HK:
+            grad_out(n)
         terms(*group)
-        first_sends(*group)
         if n >= 2:
             join_sends(*GROUPS[n - 2])
         if n >= 4:
             y_total(*GROUPS[n - 4])
 
-    outs = []
-
-    def put(src, dst, n):
-        c = pltpu.make_async_copy(src, dst, out_sem.at[n])
-        c.start()
-        outs.append(c)
-
     for n in (6, 7):
         join_sends(*GROUPS[n])
     y_total(*GROUPS[4])
     for h in range(HK):
-        gr_v[0, :, h * D:(h + 1) * D] = key_grad(h, 4).astype(BF16)
-        gr_v[1, :, h * D:(h + 1) * D] = value_grad(h, 4).astype(BF16)
-    put(gr_v.at[0], grk_hbm, 1)
-    put(gr_v.at[1], grv_hbm, 2)
+        grk_out[:, h * D:(h + 1) * D] = key_grad(h, 4).astype(BF16)
+        grv_out[:, h * D:(h + 1) * D] = value_grad(h, 4).astype(BF16)
 
     def query_grad(h):
-        def body(j, _):
-            gq_v[h, j] = (dot_n(kvt[0, h], ds[h, j]) * SCALE).T.astype(BF16)
-            return 0
-
-        lax.fori_loop(0, NJ, body, 0, unroll=True)
-        for i in range(8):
-            n = h * 8 + i
-            put(gq_v.at[h, i // 2, (i % 2) * 128:(i % 2 + 1) * 128, :],
-                gq_hbm.at[:, n * D:(n + 1) * D], 5 + n)
+        for j in range(NJ):
+            d = (dot_n(kvt[0, h], ds[h, j]) * SCALE).T.astype(BF16)
+            for i in range(2):
+                n = h * 8 + j * 2 + i
+                gq_out[:, n * D:(n + 1) * D] = d[i * 128:(i + 1) * 128]
 
     y_total(*GROUPS[5])
-    query_grad(0)
-    query_grad(1)
+    for h in range(HK):
+        for ci in range(5):
+            turn_keys(0, h, ci)
+        query_grad(h)
+    objective = jnp.minimum(ratio * adv, clipped * adv)
+    loss_s[0] = -jnp.sum(token_scale * importance * objective)
+    loss_out = pltpu.make_async_copy(loss_s, loss_hbm, out_sem.at[0])
+    loss_out.start()
     for h in range(HK):
         y_total(OWN, h)
     for h in range(HK):
@@ -408,26 +419,18 @@
             total = ownz[t, OWN, h]
             for b in range(3):
                 total = total + zr[b, h, t].astype(F32)
-            gp_v[t, :, h * D:(h + 1) * D] = total.astype(BF16)
-    put(gp_v.at[1], gpk_hbm, 3)
-    put(gp_v.at[0], gpv_hbm, 4)
+            (gpv_out, gpk_out)[t][:, h * D:(h + 1) * D] = total.astype(BF16)
     loss_out.wait()
-    for c in outs:
-        c.wait()
     for c in sends:
         c.wait_send()
 
 
 def hand_over(*refs):
-    held, sem = refs[12:18], refs[18]
-    loads = [pltpu.make_async_copy(refs[n], held[n], sem.at[0, n]) for n in range(6)]
-    stores = [pltpu.make_async_copy(held[n], refs[6 + n], sem.at[1, n]) for n in range(6)]
-    for c in loads:
+    sem = refs[-1]
+    copies = [pltpu.make_async_copy(refs[n], refs[6 + n], sem.at[n]) for n in range(6)]
+    for c in copies:
         c.start()
-    for n in range(6):
-        loads[n].wait()
-        stores[n].start()
-    for c in stores:
+    for c in copies:
         c.wait()
 
 
@@ -437,18 +440,19 @@
     dma = pltpu.SemaphoreType.DMA
     vm = pltpu.VMEM
     mpn = lax.axis_size("mp")
+    fixed = functools.partial(pltpu.with_memory_space_constraint, memory_space=pltpu.HBM)
     outs = pl.pallas_call(
         kernel,
         out_shape=(
-            jax.ShapeDtypeStruct(q.shape, BF16),
-            jax.ShapeDtypeStruct(rk.shape, BF16),
-            jax.ShapeDtypeStruct(rv.shape, BF16),
-            jax.ShapeDtypeStruct(pk.shape, BF16),
-            jax.ShapeDtypeStruct(pv.shape, BF16),
+            pltpu.VMEM(q.shape, BF16),
+            pltpu.VMEM(rk.shape, BF16),
+            pltpu.VMEM(rv.shape, BF16),
+            pltpu.VMEM(pk.shape, BF16),
+            pltpu.VMEM(pv.shape, BF16),
             jax.ShapeDtypeStruct((1,), F32),
         ),
         in_specs=[any_spec] * 11,
-        out_specs=(any_spec,) * 6,
+        out_specs=(pl.BlockSpec(memory_space=pltpu.VMEM),) * 5 + (any_spec,),
         scratch_shapes=[
             vm((2, HK, KEYS, D), BF16),
             vm((2, HK, D, KEYS), BF16),
@@ -456,6 +460,7 @@
             vm((HK, NJ, JR, D), BF16),
             vm((HK, NJ, D, JR), BF16),
             vm((HK, NJ, KEYS, JR), F32),
+            vm((HK, NJ, D, JR), F32),
             vm((HK, NJ, KEYS, JR), BF16),
             vm((HK, NJ, KEYS, JR), BF16),
             vm((HK, NJ, 8, JR), F32),
@@ -477,15 +482,12 @@
             vm((3, HK, 2, BK, D), BF16),
             vm((3, HK, 2, BK, D), BF16),
             vm((2, 4, HK, BK, D), F32),
-            vm((HK, NJ, JR, D), BF16),
-            vm((2, rows, HK * D), BF16),
-            vm((2, BK, HK * D), BF16),
             dma((17,)),
-            dma((21,)),
-            dma((HK, 2, 3)),
-            dma((HK, 2, 3)),
-            dma((HK, 4, 4)),
-            dma((HK, 4, 4)),
+            dma((1,)),
+            dma((2, HK, 5)),
+            dma((2, HK, 5)),
+            dma((2, HK, 4, 3)),
+            dma((2, HK, 4, 3)),
             dma((max(mpn - 1, 1),)),
             dma((max(mpn - 1, 1),)),
             dma((2, 4, HK)),
@@ -496,21 +498,19 @@
             dma((3, HK)),
         ],
         compiler_params=pltpu.CompilerParams(
-            collective_id=0, has_side_effects=True, vmem_limit_bytes=63 * 1024 * 1024
+            collective_id=0, has_side_effects=True, vmem_limit_bytes=48 * 1024 * 1024
         ),
         name="attention_gradient",
-    )(q, rk, rv, pk, pv, ro, prox.reshape(1, rows), beh.reshape(1, rows), adv, lens,
-      mask.reshape(1, rows))
+    )(*[fixed(a) for a in (q, rk, rv, pk, pv, ro, prox.reshape(1, rows), beh.reshape(1, rows))],
+      adv, lens, fixed(mask.reshape(1, rows)))
     return pl.pallas_call(
         hand_over,
-        out_shape=tuple(jax.ShapeDtypeStruct(o.shape, o.dtype) for o in outs),
-        in_specs=[any_spec] * 6,
+        out_shape=tuple(pltpu.HBM(o.shape, o.dtype) for o in outs),
+        in_specs=[pl.BlockSpec(memory_space=pltpu.VMEM)] * 5 + [any_spec],
         out_specs=(any_spec,) * 6,
-        scratch_shapes=[vm(o.shape, o.dtype) for o in outs[:5]]
-        + [pltpu.SMEM((1,), F32), dma((2, 6))],
-        compiler_params=pltpu.CompilerParams(vmem_limit_bytes=63 * 1024 * 1024),
+        scratch_shapes=[dma((6,))],
         name="hand_over",
-    )(*outs)
+    )(*[pltpu.with_memory_space_constraint(o, pltpu.VMEM) for o in outs[:5]], outs[5])
 
 
 def solution(mesh):

time: 53.5 us -> 49.8 us (0.931)
  Pallas kernels: 51.4 us -> 47.3 us
    pallas_call x2, Pallas kernels: 51.4 us -> 47.3 us  [the longest x1 45.9 us: per_device(): pl.pallas_call(kernel, out_shape=(pltpu.VMEM(q.shape, BF16), pltpu.VMEM(r...]
where the time goes in v2:
time: 49.8 us; the launch traced here: 49.3 us
  Pallas kernels  47.3 us (95%)
  between operations  1.93 us (4%)
    pallas_call x1, Pallas kernels, per_device(): pl.pallas_call(kernel, out_shape=(pltpu.VMEM(q.shape, BF16), pltpu.VMEM(r...  45.9 us
    pallas_call x1, Pallas kernels, per_device(): pl.pallas_call(hand_over, out_shape=tuple((pltpu.HBM(o.shape, o.dtype) fo...  1.45 us

profile of v2, /device:TPU:4, one launch (start us, length us, event | category | flops | bytes accessed | tf_op | source)
XLA Modules:
  0.0 49.3 jit_solution(9142941494419382249)
XLA Ops:
  1.9 45.9 %attention_gradient.1 = (bf16[128,2048]{1,0:T(8,128)(2,1)S(1)}, bf16[128,256]{1,0:T(8,128)(2,1)S(1)}, bf16[128,256]{1,0:T(8,128)(2,1)S(1)}, bf16[64,256]{1,0:T(8...) custom-call(bf16[128,2048]{1,0:T(8,128)(2,1)} %q_hbm.1, bf16[128,256]{1,0:T(8,128)(2,1)} %rk_hbm.1, ...), custom_call_target="tpu_custom_call" | custom-call | tf_op jit(solution)/shard_map/attention_gradient/pallas_call | solution.py:444
  47.8 1.5 %hand_over.1 = (bf16[128,2048]{1,0:T(8,128)(2,1)}, bf16[128,256]{1,0:T(8,128)(2,1)}, bf16[128,256]{1,0:T(8,128)(2,1)}, bf16[64,256]{1,0:T(8,128)(2,1)}, bf16[64,256]{1,0:T(8,128)(2,1)}, /*index=5*/f32[1]{0:T(128)}) custom-call(bf16[128,2048]{1,0:T(8,128)(2,1)S(1)} %get-tuple-element.12.refs_0_, bf16[128,256]{1,0:T(8,128)(2,1)S(1)} %get-tuple-element.13.refs_1_, ...), custom_call_target="tpu_custom_call" | custom-call | tf_op jit(solution)/shard_map/hand_over/pallas_call | solution.py:506

commit v3 on v2

--- a/solution.py
+++ b/solution.py
@@ -119,6 +119,10 @@
         c.start()
         sends.append(c)
 
+    def settle():
+        while sends:
+            sends.pop(0).wait_send()
+
     def arrived(dst, rsem):
         pltpu.make_async_remote_copy(
             src_ref=dst, dst_ref=dst, send_sem=rsem, recv_sem=rsem, device_id=y_up, device_id_type=MESH
@@ -279,6 +283,7 @@
         send(lpx.at[mp], lpx.at[mp], lp_s.at[k], lp_r.at[k], mate)
     for c in small:
         c.wait()
+    settle()
     for k in range(mpn - 1):
         src = lax.rem(mp + mpn - 1 - k, mpn)
         arrived(lpx.at[src], lp_r.at[k])
@@ -337,14 +342,20 @@
         v = value_grad(h, dz)
         y2s[0, dz, h] = v[rows_of(FAR)].astype(BF16)
         y1s[1, 0, dz, h] = v[rows_of(DOWN)].astype(BF16)
+        if dz in DIRECT:
+            y1s[0, 0, dz, h] = v[rows_of(UP)].astype(BF16)
+        else:
+            joins[0, dz, h] = v[rows_of(UP)]
         first_sends(0, dz, h)
-        joins[0, dz, h] = v[rows_of(UP)]
         ownz[0, dz, h] = v[rows_of(OWN)]
         k = key_grad(h, dz)
         y2s[1, dz, h] = k[rows_of(FAR)].astype(BF16)
         y1s[0, 1, dz, h] = k[rows_of(UP)].astype(BF16)
+        if dz in DIRECT:
+            y1s[1, 1, dz, h] = k[rows_of(DOWN)].astype(BF16)
+        else:
+            joins[1, dz, h] = k[rows_of(DOWN)]
         first_sends(1, dz, h)
-        joins[1, dz, h] = k[rows_of(DOWN)]
         ownz[1, dz, h] = k[rows_of(OWN)]
 
     def y1_send(way, t, dz, h):
@@ -352,11 +363,16 @@
              y1_s.at[way, t, dz, h], y1_rs.at[way, t, dz, h], y_up if way == 0 else y_dn)
 
     def first_sends(t, dz, h):
+        straight = dz in DIRECT
         send(y2s.at[t, dz, h], y2r.at[t, dz, h],
-             y2_s.at[t, dz, h], y2_rs.at[t, dz, h], (y_up, y_dn)[t])
+             y2_s.at[t, dz, h], y2_rs.at[t, dz, h], y_far if straight else (y_up, y_dn)[t])
         y1_send(1 - t, t, dz, h)
+        if straight:
+            y1_send(t, t, dz, h)
 
     def join_sends(dz, h):
+        if dz in DIRECT:
+            return
         for t in range(2):
             arrived(y2r.at[t, dz, h], y2_rs.at[t, dz, h])
             y1s[t, t, dz, h] = (joins[t, dz, h] + y2r[t, dz, h].astype(F32)).astype(BF16)
@@ -369,6 +385,9 @@
             total = ownz[t, dz, h] + (
                 y1r[0, t, dz, h].astype(F32) + y1r[1, t, dz, h].astype(F32)
             )
+            if dz in DIRECT:
+                arrived(y2r.at[t, dz, h], y2_rs.at[t, dz, h])
+                total = total + y2r[t, dz, h].astype(F32)
             if dz == OWN:
                 ownz[t, dz, h] = total
             else:
@@ -377,6 +396,7 @@
             send(zs.at[dz - 1, h], zr.at[dz - 1, h], z_s.at[dz - 1, h], z_rs.at[dz - 1, h],
                  (z_up, z_dn, z_far)[dz - 1])
 
+    DIRECT = (FAR,)
     GROUPS = ((FAR, 0), (FAR, 1), (UP, 0), (DOWN, 0), (UP, 1), (DOWN, 1), (OWN, 0), (OWN, 1))
     for n, group in enumerate(GROUPS):
         if n < HK:
@@ -384,11 +404,12 @@
         terms(*group)
         if n >= 2:
             join_sends(*GROUPS[n - 2])
-        if n >= 4:
-            y_total(*GROUPS[n - 4])
+        if n >= 5:
+            y_total(*GROUPS[n - 5])
 
     for n in (6, 7):
         join_sends(*GROUPS[n])
+    y_total(*GROUPS[3])
     y_total(*GROUPS[4])
     for h in range(HK):
         grk_out[:, h * D:(h + 1) * D] = key_grad(h, 4).astype(BF16)
@@ -412,6 +433,7 @@
     loss_out.start()
     for h in range(HK):
         y_total(OWN, h)
+    settle()
     for h in range(HK):
         for b in (2, 0, 1):
             arrived(zr.at[b, h], z_rs.at[b, h])
@@ -421,8 +443,7 @@
                 total = total + zr[b, h, t].astype(F32)
             (gpv_out, gpk_out)[t][:, h * D:(h + 1) * D] = total.astype(BF16)
     loss_out.wait()
-    for c in sends:
-        c.wait_send()
+    settle()
 
 
 def hand_over(*refs):

time: 49.8 us -> 49.2 us (0.988)
  Pallas kernels: 47.3 us -> 46.8 us
    pallas_call x1, Pallas kernels: 45.9 us -> 45.4 us  [per_device(): pl.pallas_call(kernel, out_shape=(pltpu.VMEM(q.shape, BF16), pltpu.VMEM(r...]
where the time goes in v3:
time: 49.2 us; the launch traced here: 48.8 us
  Pallas kernels  46.8 us (95%)
  between operations  1.93 us (4%)
    pallas_call x1, Pallas kernels, per_device(): pl.pallas_call(kernel, out_shape=(pltpu.VMEM(q.shape, BF16), pltpu.VMEM(r...  45.4 us
    pallas_call x1, Pallas kernels, per_device(): pl.pallas_call(hand_over, out_shape=tuple((pltpu.HBM(o.shape, o.dtype) fo...  1.45 us

profile of v3, /device:TPU:4, one launch (start us, length us, event | category | flops | bytes accessed | tf_op | source)
XLA Modules:
  0.0 48.8 jit_solution(16846207118751723915)
XLA Ops:
  1.9 45.4 %attention_gradient.1 = (bf16[128,2048]{1,0:T(8,128)(2,1)S(1)}, bf16[128,256]{1,0:T(8,128)(2,1)S(1)}, bf16[128,256]{1,0:T(8,128)(2,1)S(1)}, bf16[64,256]{1,0:T(8...) custom-call(bf16[128,2048]{1,0:T(8,128)(2,1)} %q_hbm.1, bf16[128,256]{1,0:T(8,128)(2,1)} %rk_hbm.1, ...), custom_call_target="tpu_custom_call" | custom-call | tf_op jit(solution)/shard_map/attention_gradient/pallas_call | solution.py:465
  47.3 1.5 %hand_over.1 = (bf16[128,2048]{1,0:T(8,128)(2,1)}, bf16[128,256]{1,0:T(8,128)(2,1)}, bf16[128,256]{1,0:T(8,128)(2,1)}, bf16[64,256]{1,0:T(8,128)(2,1)}, bf16[64,256]{1,0:T(8,128)(2,1)}, /*index=5*/f32[1]{0:T(128)}) custom-call(bf16[128,2048]{1,0:T(8,128)(2,1)S(1)} %get-tuple-element.12.refs_0_, bf16[128,256]{1,0:T(8,128)(2,1)S(1)} %get-tuple-element.13.refs_1_, ...), custom_call_target="tpu_custom_call" | custom-call | tf_op jit(solution)/shard_map/hand_over/pallas_call | solution.py:527

commit v4 on v3

--- a/solution.py
+++ b/solution.py
@@ -37,7 +37,7 @@
 
 def kernel(
     q_hbm, rk_hbm, rv_hbm, pk_hbm, pv_hbm, ro_hbm, prox_hbm, beh_hbm, adv_hbm, len_hbm, mask_hbm,
-    gq_out, grk_out, grv_out, gpk_out, gpv_out, loss_hbm,
+    gq_out, grk_out, grv_out, gpk_out, gpv_out, loss_out,
     kv, kvt, qs, rs, rst, es, att, pb, ds, ms, ls, fs, hds, do,
     lpx, tok, tokm, adv_s, len_s, loss_s,
     y2s, y2r, y1s, y1r, joins, zs, zr, ownz,
@@ -428,9 +428,7 @@
             turn_keys(0, h, ci)
         query_grad(h)
     objective = jnp.minimum(ratio * adv, clipped * adv)
-    loss_s[0] = -jnp.sum(token_scale * importance * objective)
-    loss_out = pltpu.make_async_copy(loss_s, loss_hbm, out_sem.at[0])
-    loss_out.start()
+    loss_out[0] = -jnp.sum(token_scale * importance * objective)
     for h in range(HK):
         y_total(OWN, h)
     settle()
@@ -442,7 +440,6 @@
             for b in range(3):
                 total = total + zr[b, h, t].astype(F32)
             (gpv_out, gpk_out)[t][:, h * D:(h + 1) * D] = total.astype(BF16)
-    loss_out.wait()
     settle()
 
 
@@ -470,10 +467,11 @@
             pltpu.VMEM(rv.shape, BF16),
             pltpu.VMEM(pk.shape, BF16),
             pltpu.VMEM(pv.shape, BF16),
-            jax.ShapeDtypeStruct((1,), F32),
+            pltpu.SMEM((1,), F32),
         ),
         in_specs=[any_spec] * 11,
-        out_specs=(pl.BlockSpec(memory_space=pltpu.VMEM),) * 5 + (any_spec,),
+        out_specs=(pl.BlockSpec(memory_space=pltpu.VMEM),) * 5
+        + (pl.BlockSpec(memory_space=pltpu.SMEM),),
         scratch_shapes=[
             vm((2, HK, KEYS, D), BF16),
             vm((2, HK, D, KEYS), BF16),
@@ -527,7 +525,7 @@
     return pl.pallas_call(
         hand_over,
         out_shape=tuple(pltpu.HBM(o.shape, o.dtype) for o in outs),
-        in_specs=[pl.BlockSpec(memory_space=pltpu.VMEM)] * 5 + [any_spec],
+        in_specs=[pl.BlockSpec(memory_space=pltpu.VMEM)] * 5 + [pl.BlockSpec(memory_space=pltpu.SMEM)],
         out_specs=(any_spec,) * 6,
         scratch_shapes=[dma((6,))],
         name="hand_over",

time: 49.2 us -> 48.6 us (0.988)
  Pallas kernels: 46.8 us -> 46.3 us
    pallas_call x1, Pallas kernels: 1.45 us -> 0.91 us  [per_device(): pl.pallas_call(hand_over, out_shape=tuple((pltpu.HBM(o.shape, o.dtype) fo...]
where the time goes in v4:
time: 48.6 us; the launch traced here: 48.2 us
  Pallas kernels  46.3 us (95%)
  between operations  1.93 us (4%)
    pallas_call x1, Pallas kernels, per_device(): pl.pallas_call(kernel, out_shape=(pltpu.VMEM(q.shape, BF16), pltpu.VMEM(r...  45.4 us

profile of v4, /device:TPU:4, one launch (start us, length us, event | category | flops | bytes accessed | tf_op | source)
XLA Modules:
  0.0 48.2 jit_solution(10189417350066517779)
XLA Ops:
  1.9 45.4 %attention_gradient.1 = (bf16[128,2048]{1,0:T(8,128)(2,1)S(1)}, bf16[128,256]{1,0:T(8,128)(2,1)S(1)}, bf16[128,256]{1,0:T(8,128)(2,1)S(1)}, bf16[64,256]{1,0:T(8...) custom-call(bf16[128,2048]{1,0:T(8,128)(2,1)} %q_hbm.1, bf16[128,256]{1,0:T(8,128)(2,1)} %rk_hbm.1, ...), custom_call_target="tpu_custom_call" | custom-call | tf_op jit(solution)/shard_map/attention_gradient/pallas_call | solution.py:462
  47.3 0.9 %hand_over.1 = (bf16[128,2048]{1,0:T(8,128)(2,1)}, bf16[128,256]{1,0:T(8,128)(2,1)}, bf16[128,256]{1,0:T(8,128)(2,1)}, bf16[64,256]{1,0:T(8,128)(2,1)}, bf16[64,256]{1,0:T(8,128)(2,1)}, /*index=5*/f32[1]{0:T(128)}) custom-call(bf16[128,2048]{1,0:T(8,128)(2,1)S(1)} %get-tuple-element.12.refs_0_, bf16[128,256]{1,0:T(8,128)(2,1)S(1)} %get-tuple-element.13.refs_1_, ...), custom_call_target="tpu_custom_call" | custom-call | tf_op jit(solution)/shard_map/hand_over/pallas_call | solution.py:525
